TPU v7x, 32 devices: a whole 2x2x4 slice. The times are simulated.
32 devices in a mesh: dp: 8 (over y, x, core), seq: 4 (over z).
Axes of the slice: x: 2, y: 2, z: 4, core: 2. Of those that a mesh axis runs over, the one named last changes fastest.
Arguments:
- tokens: bfloat16 [96, 320, 768], P('dp', 'seq'), may hold values from -6 to 6
- lengths: int32 [96], P('dp'), may hold values from 197 to 577, as said below
- grad_out: bfloat16 [96, 320, 768], P('dp', 'seq'), may hold values from -6 to 6
- query_weight: bfloat16 [768, 768], replicated, may hold values from -0.4375 to 0.4375
- query_bias: bfloat16 [768], replicated, may hold values from -1.796875 to 1.796875
- key_weight: bfloat16 [768, 768], replicated, may hold values from -0.21875 to 0.21875
- value_weight: bfloat16 [768, 768], replicated, may hold values from -0.21875 to 0.21875
- value_bias: bfloat16 [768], replicated, may hold values from -1.796875 to 1.796875
- output_weight: bfloat16 [768, 768], replicated, may hold values from -0.875 to 0.875
- output_bias: bfloat16 [768], replicated, may hold values from -1.796875 to 1.796875
- up_weight: bfloat16 [768, 3072], replicated, may hold values from -0.21875 to 0.21875
- up_bias: bfloat16 [3072], replicated, may hold values from -1.796875 to 1.796875
- down_weight: bfloat16 [3072, 768], replicated, may hold values from -0.21875 to 0.21875
- down_bias: bfloat16 [768], replicated, may hold values from -1.796875 to 1.796875
- first_gain: bfloat16 [768], replicated, may hold values from 0.5 to 1.5
- first_shift: bfloat16 [768], replicated, may hold values from -1.796875 to 1.796875
- second_gain: bfloat16 [768], replicated, may hold values from 0.5 to 1.5
- second_shift: bfloat16 [768], replicated, may hold values from -1.796875 to 1.796875
- router_weight: bfloat16 [768], replicated, may hold values from -0.21875 to 0.21875
Outputs:
- mixed: bfloat16 [96, 320, 768], P('dp', 'seq')
- tokens_grad: bfloat16 [96, 320, 768], P('dp', 'seq')
- grad_query_weight: float32 [768, 768], replicated
- grad_query_bias: float32 [768], replicated
- grad_key_weight: float32 [768, 768], replicated
- grad_value_weight: float32 [768, 768], replicated
- grad_value_bias: float32 [768], replicated
- grad_output_weight: float32 [768, 768], replicated
- grad_output_bias: float32 [768], replicated
- grad_up_weight: float32 [768, 3072], replicated
- grad_up_bias: float32 [3072], replicated
- grad_down_weight: float32 [3072, 768], replicated
- grad_down_bias: float32 [768], replicated
- grad_first_gain: float32 [768], replicated
- grad_first_shift: float32 [768], replicated
- grad_second_gain: float32 [768], replicated
- grad_second_shift: float32 [768], replicated
- grad_router_weight: float32 [768], replicated
Inputs may be any that keep to these rules, and one draw needn't show every extreme that they name: `lengths`: each length is 197 or 577; each run of 12 images of one dp index holds at least one of length 577.
All inputs are finite; a program needn't handle non-finite values.
Results may differ from a plain program's by a relative error of at most 0.019.
Values may be sent and summed in bfloat16 or wider, within the bound.
No kernel may reach another device: no remote copies, remote signals or barrier semaphores. Data moves between devices by JAX's collectives and lax.ppermute only.
A program may use at most 256 MiB of HBM per device.

v0:
```python
import functools
import math

import jax
import jax.numpy as jnp
from jax import lax
from jax.experimental import pallas as pl
from jax.experimental.pallas import tpu as pltpu
from jax.sharding import PartitionSpec as P

HEADS = 12
HEAD_DIM = 64
EPSILON = 1e-06
PAIR = 2 * HEAD_DIM
LANES = 128
SCALE = HEAD_DIM ** (-0.5)
SCORE_FACTOR = SCALE * math.log2(math.e)
ROOT_HALF = math.sqrt(0.5)
DENSITY = 1.0 / math.sqrt(2.0 * math.pi)
BELL = -0.5 * math.log2(math.e)
MASKED = -1e30
TILE = 512
MIB = 1024 * 1024
F32 = jnp.float32
BF16 = jnp.bfloat16

QB, VB, OB, G1, S1, G2, S2, RW, DB = range(9)


def cost(microseconds):
    return pl.CostEstimate(
        flops=microseconds * 1_150_000_000, bytes_accessed=1_000_000, transcendentals=0
    )


def nn(a, b):
    return lax.dot_general(a, b, (((1,), (0,)), ((), ())), preferred_element_type=F32)


def nt(a, b):
    return lax.dot_general(a, b, (((1,), (1,)), ((), ())), preferred_element_type=F32)


def tn(a, b):
    return lax.dot_general(a, b, (((0,), (0,)), ((), ())), preferred_element_type=F32)


def hat(field):
    mean = jnp.mean(field, axis=-1, keepdims=True)
    centred = field - mean
    spread = jnp.mean(centred * centred, axis=-1, keepdims=True)
    scale = lax.rsqrt(spread + EPSILON)
    return centred * scale, scale


def hat_back(grad, normal, scale):
    first = jnp.mean(grad, axis=-1, keepdims=True)
    second = jnp.mean(grad * normal, axis=-1, keepdims=True)
    return scale * (grad - first - normal * second)


def row_sum(field):
    return jnp.sum(field, axis=0, keepdims=True)


def head_masks():
    lane = lax.broadcasted_iota(jnp.int32, (1, PAIR), 1)
    return [
        jnp.where(lane < HEAD_DIM, 1.0, 0.0).astype(BF16),
        jnp.where(lane < HEAD_DIM, 0.0, 1.0).astype(BF16),
    ]


def block_at(me, distance, size):
    return pl.ds(pl.multiple_of(jnp.bitwise_xor(me, distance) * size, 16), size)


def attention_kernel(info, *refs, parts):
    came, (vec, wq, wk, wv, wo) = refs[:parts], refs[parts : parts + 5]
    (
        x_ref,
        normed_ref,
        q_ref,
        k_ref,
        v_ref,
        ctx_ref,
        middle_ref,
        one_ref,
        second_ref,
        gate_ref,
        row_ref,
        lse_ref,
    ) = refs[-12:]
    slots = x_ref.shape[1]
    size = slots // parts
    count = info[1 + pl.program_id(0)]
    for distance in range(parts):
        x_ref[0, block_at(info[0], distance, size), :] = came[distance][0]
    x = x_ref[0].astype(F32)
    normal, _ = hat(x)
    normed = (normal * vec[G1 : G1 + 1] + vec[S1 : S1 + 1]).astype(BF16)
    normed_ref[0] = normed
    logit = jnp.sum(normed.astype(F32) * vec[RW : RW + 1], axis=-1, keepdims=True)
    gate = jax.nn.sigmoid(logit)
    inside = lax.broadcasted_iota(jnp.int32, (slots, 1), 0) < count
    row = jnp.where(inside, gate, 0.0)
    gate_ref[0] = jnp.broadcast_to(gate, (slots, LANES))
    row_ref[0] = jnp.broadcast_to(row, (slots, LANES))
    q_ref[0] = (nn(normed, wq[...]) + vec[QB : QB + 1]).astype(BF16)
    k_ref[0] = nn(normed, wk[...]).astype(BF16)
    v_ref[0] = (nn(normed, wv[...]) + vec[VB : VB + 1]).astype(BF16)
    key_mask = jnp.where(
        lax.broadcasted_iota(jnp.int32, (1, slots), 1) < count, 0.0, MASKED
    )
    masks = head_masks()
    lane = lax.broadcasted_iota(jnp.int32, (1, LANES), 1)
    ones = jnp.ones((slots, LANES), BF16)
    lse = jnp.zeros((slots, LANES), F32)
    for pair in range(HEADS // 2):
        at = slice(pair * PAIR, (pair + 1) * PAIR)
        queries = q_ref[0, :, at]
        keys = k_ref[0, :, at]
        values = jnp.concatenate([v_ref[0, :, at], ones], axis=1)
        halves = []
        for e in range(2):
            scores = nt(queries * masks[e], keys) * SCORE_FACTOR + key_mask
            top = jnp.max(scores, axis=-1, keepdims=True)
            expo = jnp.exp2(scores - top).astype(BF16)
            mixed = nn(expo, values)
            total = mixed[:, PAIR:]
            halves.append(mixed[:, :PAIR] / total)
            lse = jnp.where(lane == 2 * pair + e, top + jnp.log2(total), lse)
        low = jnp.where(lane < HEAD_DIM, halves[0], halves[1])
        ctx_ref[0, :, at] = low.astype(BF16)
    lse_ref[0] = lse
    one = nn(ctx_ref[0], wo[...]) + vec[OB : OB + 1]
    one_ref[0] = one.astype(BF16)
    middle = x + row * one
    middle_ref[0] = middle
    again, _ = hat(middle)
    second_ref[0] = (again * vec[G2 : G2 + 1] + vec[S2 : S2 + 1]).astype(BF16)


def run_attention(info, own, came, vectors, weights):
    parts = 1 + len(came)
    images, size, width = came[0].shape
    slots = parts * size
    whole = lambda a: pl.BlockSpec(a.shape, lambda i, c: (0,) * a.ndim)
    outs = [(width, BF16)] * 6 + [(width, F32)] + [(width, BF16)] * 2 + [(LANES, F32)] * 3
    return pl.pallas_call(
        functools.partial(attention_kernel, parts=parts),
        grid_spec=pltpu.PrefetchScalarGridSpec(
            num_scalar_prefetch=1,
            grid=(images,),
            in_specs=[pl.BlockSpec((1, size, width), lambda i, c: (c[0] * images + i, 0, 0))]
            + [pl.BlockSpec((1, size, width), lambda i, c: (i, 0, 0))] * len(came)
            + [whole(a) for a in (vectors, *weights)],
            out_specs=[pl.BlockSpec((1, slots, lanes), lambda i, c: (i, 0, 0)) for lanes, _ in outs],
        ),
        out_shape=[jax.ShapeDtypeStruct((images, slots, lanes), t) for lanes, t in outs],
        compiler_params=pltpu.CompilerParams(vmem_limit_bytes=20 * MIB),
        cost_estimate=cost(20),
        name="attention_forward",
    )(info, own, *came, vectors, *weights)


def feed_kernel(info, second, row, up, bias, down, middle, one, gate, vec, *refs, images):
    parts = (len(refs) - 15) // 2
    came, refs = refs[:parts], refs[parts:]
    mixed, refs = refs[:parts], refs[parts:]
    back_sum, total_ref, low_ref, logit_ref, sums, down_send, down_keep, up_send, up_keep = refs[:9]
    bias_grad, back, flipped, two, pulled, grad_out = refs[9:]
    step = pl.program_id(0)
    size = came[0].shape[1]
    slots = parts * size

    def rows_of(image, distance):
        start = jnp.bitwise_xor(info[0], distance) * size + image * slots
        return pl.ds(pl.multiple_of(start, 16), size)

    @pl.when(step == 0)
    def _():
        total = jnp.zeros(back_sum.shape, F32)
        for image in range(images):
            for distance in range(parts):
                at = rows_of(image, distance)
                upstream = came[distance][image]
                grad_out[at, :] = upstream
                value = (row[at, :1] * upstream.astype(F32)).astype(BF16)
                back[at, :] = value
                total = total + row_sum(value.astype(F32))
        back_sum[...] = total
        flipped[...] = second[...].T
        two[...] = jnp.zeros_like(two)
        pulled[...] = jnp.zeros_like(pulled)

    hidden = nn(second[...], up[...]) + bias[...]
    phi = 0.5 + 0.5 * lax.erf(hidden * ROOT_HALF)
    density = DENSITY * jnp.exp2(hidden * hidden * BELL)
    active = (hidden * phi).astype(BF16)
    slope = phi + hidden * density
    two[...] += nn(active, down[...])
    low = (nt(back[...], down[...]) * slope).astype(BF16)
    bias_grad[...] = row_sum(low.astype(F32))
    pulled[...] += nt(low, up[...])
    down_grad = tn(active, back[...]).astype(BF16)
    up_grad = nn(flipped[...], low).astype(BF16)

    @pl.when(step < pl.num_programs(0) // 2)
    def _():
        down_send[...] = down_grad
        up_send[...] = up_grad

    @pl.when(step >= pl.num_programs(0) // 2)
    def _():
        down_keep[...] = down_grad
        up_keep[...] = up_grad

    @pl.when(step == pl.num_programs(0) - 1)
    def _():
        zero = jnp.zeros((1, second.shape[1]), F32)

        def finish(image, carry):
            gain_sum, shift_sum, one_sum = carry
            for distance in range(parts):
                at = rows_of(image, distance)
                upstream = grad_out[at, :].astype(F32)
                weight = row[at, :1]
                branch_two = two[at, :] + vec[DB : DB + 1]
                centre = middle[at, :]
                mixed[distance][image] = (centre + weight * branch_two).astype(BF16)
                normal, scale = hat(centre)
                grad = pulled[at, :]
                total = hat_back(grad * vec[G2 : G2 + 1], normal, scale) + upstream
                total_ref[at, :] = total.astype(BF16)
                low = (weight * total).astype(BF16)
                low_ref[at, :] = low
                gated = jnp.sum(
                    upstream * branch_two + total * one[at, :].astype(F32), axis=-1, keepdims=True
                )
                logit_ref[at, :] = weight * (1.0 - gate[at, :]) * gated
                gain_sum = gain_sum + row_sum(grad * normal)
                shift_sum = shift_sum + row_sum(grad)
                one_sum = one_sum + row_sum(low.astype(F32))
            return gain_sum, shift_sum, one_sum

        gain_sum, shift_sum, one_sum = lax.fori_loop(0, images, finish, (zero, zero, zero))
        sums[0:1] = gain_sum
        sums[1:2] = shift_sum
        sums[2:3] = one_sum


def shared_out(tiles, step):
    return jnp.minimum(step, tiles - 1), jnp.maximum(step - tiles, 0)


def run_feed(info, second, row, up, bias, down, middle, one, gate, vectors, images, came):
    rows, width = second.shape
    units = up.shape[1]
    tiles = units // TILE // 2
    parts = len(came)
    size = rows // images // parts
    once = dict(pipeline_mode=pl.Buffered(1))
    whole = lambda a, **mode: pl.BlockSpec(a.shape, lambda t, c: (0,) * len(a.shape), **mode)
    tile = lambda t, c: lax.rem(t + (1 - c[1]) * tiles, 2 * tiles)
    shape = jax.ShapeDtypeStruct
    field = lambda dtype: shape((rows, width), dtype)
    outs = [shape((images, size, width), BF16)] * parts
    outs += [shape((1, width), F32), field(BF16), field(BF16), shape(row.shape, F32)]
    outs += [shape((8, width), F32)]
    scratch = [pltpu.VMEM((rows, width), BF16), pltpu.VMEM((width, rows), BF16)]
    scratch += [pltpu.VMEM((rows, width), F32)] * 2 + [pltpu.VMEM((rows, width), BF16)]
    return pl.pallas_call(
        functools.partial(feed_kernel, images=images),
        grid_spec=pltpu.PrefetchScalarGridSpec(
            num_scalar_prefetch=1,
            grid=(2 * tiles,),
            in_specs=[
                whole(second, **once),
                whole(row, **once),
                pl.BlockSpec((width, TILE), lambda t, c: (0, tile(t, c))),
                pl.BlockSpec((1, TILE), lambda t, c: (0, tile(t, c))),
                pl.BlockSpec((TILE, width), lambda t, c: (tile(t, c), 0)),
            ]
            + [whole(a, **once) for a in (middle, one, gate, vectors)]
            + [pl.BlockSpec((images,) + came[0].shape[1:], lambda t, c: (c[0], 0, 0), **once)]
            + [whole(a, **once) for a in came[1:]],
            out_specs=[whole(o, **once) for o in outs]
            + [
                pl.BlockSpec((TILE, width), lambda t, c, n=n: (shared_out(tiles, t)[n], 0))
                for n in range(2)
            ]
            + [
                pl.BlockSpec((width, TILE), lambda t, c, n=n: (0, shared_out(tiles, t)[n]))
                for n in range(2)
            ]
            + [pl.BlockSpec((1, TILE), lambda t, c: (0, tile(t, c)))],
            scratch_shapes=scratch,
        ),
        out_shape=outs
        + [shape((units // 2, width), BF16)] * 2
        + [shape((width, units // 2), BF16)] * 2
        + [shape((1, units), F32)],
        compiler_params=pltpu.CompilerParams(vmem_limit_bytes=34 * MIB),
        cost_estimate=cost(43),
        name="feed",
    )(info, second, row, up, bias, down, middle, one, gate, vectors, *came)


def attention_back_kernel(
    info,
    x_ref,
    q_ref,
    k_ref,
    v_ref,
    lse_ref,
    grad_one,
    grad_middle,
    grad_logit,
    normed,
    vec,
    wq,
    wk,
    wv,
    wo,
    *rest,
    image,
    parts,
):
    grads, *tokens_grad, sums, pulled, tokens_back = rest[-5 - parts + 1 :]
    slots = x_ref.shape[1]
    count = info[1 + image]
    pulled[...] = nt(grad_one[0], wo[...]).astype(BF16)
    lse = lse_ref[0].T
    inside = lax.broadcasted_iota(jnp.int32, (slots, 1), 0) < count
    masks = head_masks()
    for pair in range(HEADS // 2):
        at = slice(pair * PAIR, (pair + 1) * PAIR)
        queries, keys, values = q_ref[0, :, at], k_ref[0, :, at], v_ref[0, :, at]
        above = pulled[:, at]
        grad_q = grad_k = grad_v = None
        for e in range(2):
            h = 2 * pair + e
            own_keys = keys * masks[e]
            scores = nt(own_keys, queries) * SCORE_FACTOR - lse[h : h + 1]
            probs = jnp.exp2(jnp.where(inside, scores, MASKED))
            slope = probs * nt(values * masks[e], above)
            centre = row_sum(slope)
            low = (slope - probs * centre).astype(BF16)
            terms = (
                tn(low, own_keys),
                nn(low, queries * masks[e]),
                nn(probs.astype(BF16), above * masks[e]),
            )
            if e == 0:
                grad_q, grad_k, grad_v = terms
            else:
                grad_q, grad_k, grad_v = (
                    grad_q + terms[0],
                    grad_k + terms[1],
                    grad_v + terms[2],
                )
        grads[0, :, at] = (grad_q * SCALE).astype(BF16)
        grads[1, :, at] = (grad_k * SCALE).astype(BF16)
        grads[2, :, at] = grad_v.astype(BF16)
    logit = grad_logit[0, :, :1]
    total = (
        nt(grads[0], wq[...])
        + nt(grads[1], wk[...])
        + nt(grads[2], wv[...])
        + logit * vec[RW : RW + 1]
    )
    normal, scale = hat(x_ref[0].astype(F32))
    sums[0:1] = row_sum(grads[0].astype(F32))
    sums[1:2] = row_sum(grads[2].astype(F32))
    sums[2:3] = row_sum(total * normal)
    sums[3:4] = row_sum(total)
    sums[4:5] = row_sum(normed[0].astype(F32) * logit)
    back = hat_back(total * vec[G1 : G1 + 1], normal, scale)
    tokens_back[...] = (back + grad_middle[0].astype(F32)).astype(BF16)
    for distance in range(parts):
        tokens_grad[distance][0] = tokens_back[block_at(info[0], distance, slots // parts), :]


def run_attention_back(image, info, fields, vectors, weights, parts):
    images, slots, width = fields[0].shape
    at = lambda a: pl.BlockSpec((1,) + a.shape[1:], lambda i, c: (image, 0, 0))
    whole = lambda a: pl.BlockSpec(a.shape, lambda i, c: (0,) * a.ndim)
    args = [*fields, vectors, *weights]
    in_specs = [at(a) for a in fields] + [whole(a) for a in (vectors, *weights)]
    shape = jax.ShapeDtypeStruct
    size = slots // parts
    return pl.pallas_call(
        functools.partial(attention_back_kernel, image=image, parts=parts),
        grid_spec=pltpu.PrefetchScalarGridSpec(
            num_scalar_prefetch=1,
            grid=(1,),
            in_specs=in_specs,
            out_specs=[pl.BlockSpec((3, slots, width), lambda i, c: (0, 0, 0))]
            + [pl.BlockSpec((1, size, width), lambda i, c: (0, 0, 0))] * parts
            + [pl.BlockSpec((8, width), lambda i, c: (0, 0))],
            scratch_shapes=[pltpu.VMEM((slots, width), BF16)] * 2,
        ),
        out_shape=[shape((3, slots, width), BF16)]
        + [shape((1, size, width), BF16)] * parts
        + [shape((8, width), F32)],
        compiler_params=pltpu.CompilerParams(vmem_limit_bytes=16 * MIB),
        cost_estimate=cost(11),
        name="attention_backward",
    )(info, *args)


def outer_kernel(info, normed, ctx, grad_one, *refs, images):
    grads, (send, keep, flipped, joined) = refs[:images], refs[images:]
    step = pl.program_id(0)
    half = pl.num_programs(0) // 2
    which = lax.rem(step + half * (1 - info[1]), 2 * half)

    @pl.when(step == 0)
    def _():
        flipped[...] = normed[...].T

    @pl.when(which < 3)
    def _():
        slots = grads[0].shape[1]
        for image in range(images):
            joined[image * slots : (image + 1) * slots] = grads[image][0]

    for out, now in ((send, step < half), (keep, step >= half)):

        @pl.when(jnp.logical_and(now, which < 3))
        def _(out=out):
            out[...] = nn(flipped[...], joined[...]).astype(BF16)

        @pl.when(jnp.logical_and(now, which == 3))
        def _(out=out):
            out[...] = tn(ctx[...], grad_one[...]).astype(BF16)


def run_outer(info, normed, ctx, grad_one, grads):
    rows, width = normed.shape
    images = len(grads)
    whole = lambda a: pl.BlockSpec(a.shape, lambda s, c: (0,) * a.ndim)
    return pl.pallas_call(
        functools.partial(outer_kernel, images=images),
        grid_spec=pltpu.PrefetchScalarGridSpec(
            num_scalar_prefetch=1,
            grid=(4,),
            in_specs=[
                whole(normed),
                whole(ctx),
                whole(grad_one),
            ]
            + [
                pl.BlockSpec(
                    (1, rows // images, width),
                    lambda s, c: (jnp.minimum(lax.rem(s + 2 * (1 - c[1]), 4), 2), 0, 0),
                )
            ]
            * images,
            out_specs=[
                pl.BlockSpec((width, width), lambda s, c, n=n: (shared_out(2, s)[n], 0))
                for n in range(2)
            ],
            scratch_shapes=[pltpu.VMEM((width, rows), BF16), pltpu.VMEM((rows, width), BF16)],
        ),
        out_shape=[jax.ShapeDtypeStruct((2 * width, width), BF16)] * 2,
        compiler_params=pltpu.CompilerParams(vmem_limit_bytes=24 * MIB),
        cost_estimate=cost(9),
        name="outer",
    )(info, normed, ctx, grad_one, *grads)


def bits_of(axis):
    size = lax.axis_size(axis)
    count = size.bit_length() - 1
    if size != 1 << count:
        raise ValueError("axis size")
    return [(axis, b) for b in range(count)]


def bit_of(step):
    axis, b = step
    return (lax.axis_index(axis) >> b) & 1


def swap(field, step):
    axis, b = step
    return lax.ppermute(field, axis, [(i, i ^ (1 << b)) for i in range(lax.axis_size(axis))])


def add_low(a, b):
    return (a.astype(F32) + b.astype(F32)).astype(BF16)


def halves(field, step):
    half = field.shape[0] // 2
    own = bit_of(step)
    return (
        lax.dynamic_slice_in_dim(field, (1 - own) * half, half),
        lax.dynamic_slice_in_dim(field, own * half, half),
    )


def ordered(own, other, step, axis=0):
    return jnp.where(
        bit_of(step) == 0,
        jnp.concatenate([own, other], axis=axis),
        jnp.concatenate([other, own], axis=axis),
    )


def spread_kernel(info, own, other, out):
    @pl.when(pl.program_id(0) == 0)
    def _():
        out[...] = own[...].astype(F32)

    @pl.when(pl.program_id(0) == 1)
    def _():
        out[...] = other[...].astype(F32)


def run_spread(info, own, other, axis):
    rows, cols = own.shape
    cuts = 2
    block = (rows // cuts, cols)
    place = lambda h, b: (b, h) if axis else (h * cuts + b, 0)
    still = cuts - 1
    return pl.pallas_call(
        spread_kernel,
        grid_spec=pltpu.PrefetchScalarGridSpec(
            num_scalar_prefetch=1,
            grid=(2, cuts),
            in_specs=[
                pl.BlockSpec(block, lambda h, b, c: (jnp.where(h == 0, b, still), 0)),
                pl.BlockSpec(block, lambda h, b, c: (jnp.where(h == 0, 0, b), 0)),
            ],
            out_specs=pl.BlockSpec(block, lambda h, b, c: place(jnp.bitwise_xor(h, c[1]), b)),
        ),
        out_shape=jax.ShapeDtypeStruct((rows * (2 - axis), cols * (1 + axis)), F32),
        compiler_params=pltpu.CompilerParams(vmem_limit_bytes=20 * MIB),
        cost_estimate=cost(7),
        name="spread",
    )(info, own, other)


def split_kernel(info, own, other, *outs, cuts):
    step = pl.program_id(0)
    for g in range(2):
        for w in range(2):
            start = (jnp.bitwise_xor(g, info[1]) * 2 + w) * cuts
            now = jnp.logical_and(step >= start, step < start + cuts)
            for source, near in ((own, step < 2 * cuts), (other, step >= 2 * cuts)):

                @pl.when(jnp.logical_and(now, near))
                def _(source=source, out=outs[2 * g + w]):
                    out[...] = source[...].astype(F32)


def run_split(info, own, other):
    rows, width = own.shape
    cuts = 1
    side = rows // 2
    block = (side // cuts, width)

    def place(t, c, g, w):
        start = (jnp.bitwise_xor(g, c[1]) * 2 + w) * cuts
        return jnp.clip(t - start, 0, cuts - 1), 0

    return pl.pallas_call(
        functools.partial(split_kernel, cuts=cuts),
        grid_spec=pltpu.PrefetchScalarGridSpec(
            num_scalar_prefetch=1,
            grid=(4 * cuts,),
            in_specs=[
                pl.BlockSpec(block, lambda t, c: (jnp.minimum(t, 2 * cuts - 1), 0)),
                pl.BlockSpec(block, lambda t, c: (jnp.maximum(t - 2 * cuts, 0), 0)),
            ],
            out_specs=[
                pl.BlockSpec(block, functools.partial(place, g=g, w=w))
                for g in range(2)
                for w in range(2)
            ],
        ),
        out_shape=[jax.ShapeDtypeStruct((side, width), F32)] * 4,
        compiler_params=pltpu.CompilerParams(vmem_limit_bytes=24 * MIB),
        cost_estimate=cost(8),
        name="split",
    )(info, own, other)


def swap_far(field, distance):
    size = lax.axis_size("seq")
    return lax.ppermute(field, "seq", [(i, i ^ distance) for i in range(size)])


class Stage:
    def __init__(self, sends, moves, finish):
        self.sends, self.moves, self.finish = sends, moves, finish


def move_by(step):
    return lambda field: swap(field, step)


def move_far(distance):
    return lambda field: swap_far(field, distance)


def scatter_stage(fields, steps):
    pieces = [halves(f, s) for f, s in zip(fields, steps)]
    return Stage(
        [p[0] for p in pieces],
        [move_by(s) for s in steps],
        lambda came: [add_low(p[1], c) for p, c in zip(pieces, came)],
    )


def gather_stage(fields, steps, axis=0):
    return Stage(
        fields,
        [move_by(s) for s in steps],
        lambda came: [ordered(f, c, s, axis) for f, c, s in zip(fields, came, steps)],
    )


def begin(stages, *gates):
    sends = [s for stage in stages for s in stage.sends]
    results = lax.optimization_barrier((*gates, *sends))
    moves = [m for stage in stages for m in stage.moves]
    came = [m(s) for m, s in zip(moves, results[len(gates) :])]
    return list(results[: len(gates)]), (stages, came)


def end(pending, *markers):
    stages, came = pending
    came = list(lax.optimization_barrier((*came, *markers))[: len(came)])
    left, results = came, []
    for stage in stages:
        count = len(stage.sends)
        results.append(stage.finish(left[:count]))
        left = left[count:]
    return (*results, came)


def exchange(*stages):
    return end(begin(stages)[1])[:-1]


def place_kernel(info, *refs, counts):
    *parts, out = refs
    at = 0
    for distance, count in enumerate(counts):

        @pl.when(pl.program_id(0) == distance)
        def _(now=parts[at : at + count]):
            rows = 0
            for part in now:
                out[rows : rows + part.shape[0]] = part[...]
                rows += part.shape[0]

        at += count


def run_place(info, parts):
    size, width = parts[0][0].shape[1:]
    images = sum(p.shape[0] for p in parts[0])
    args = [p for group in parts for p in group]
    return pl.pallas_call(
        functools.partial(place_kernel, counts=[len(group) for group in parts]),
        grid_spec=pltpu.PrefetchScalarGridSpec(
            num_scalar_prefetch=1,
            grid=(len(parts),),
            in_specs=[pl.BlockSpec(a.shape, lambda d, c: (0, 0, 0)) for a in args],
            out_specs=pl.BlockSpec(
                (images, size, width), lambda d, c: (jnp.bitwise_xor(c[0], d), 0, 0)
            ),
        ),
        out_shape=jax.ShapeDtypeStruct((len(parts) * images, size, width), BF16),
        compiler_params=pltpu.CompilerParams(vmem_limit_bytes=16 * MIB),
        cost_estimate=cost(3),
        name="place",
    )(info, *args)


def after(value, *others):
    return lax.optimization_barrier((value, *others))[0]


def on_device(
    tokens,
    lengths,
    grad_out,
    query_weight,
    query_bias,
    key_weight,
    value_weight,
    value_bias,
    output_weight,
    output_bias,
    up_weight,
    up_bias,
    down_weight,
    down_bias,
    first_gain,
    first_shift,
    second_gain,
    second_shift,
    router_weight,
):
    parts = lax.axis_size("seq")
    me = lax.axis_index("seq").astype(jnp.int32)
    group, size, width = tokens.shape
    images = group // parts
    slots = parts * size
    rows = images * slots
    distances = range(1, parts)
    blocks_for = lambda field, d: lax.dynamic_slice_in_dim(field, (me ^ d) * images, images)
    came = [swap_far(blocks_for(tokens, d), d) for d in distances]
    grad_came = [grad_out]
    for d in distances:
        grad_came.append(swap_far(after(blocks_for(grad_out, d), came[-1]), d))

    lengths = lax.dynamic_slice_in_dim(lengths, me * images, images)
    info = jnp.concatenate([me.reshape(1), (lengths + 1) // 2])
    vectors = [
        query_bias,
        value_bias,
        output_bias,
        first_gain,
        first_shift,
        second_gain,
        second_shift,
        router_weight,
        down_bias,
    ]
    vectors = jnp.pad(jnp.stack(vectors).astype(F32), ((0, 16 - len(vectors)), (0, 0)))
    flat = lambda field: field.reshape(rows, field.shape[-1])
    cube = lambda field: field.reshape(images, slots, field.shape[-1])

    weights = (query_weight, key_weight, value_weight, output_weight)
    x, normed, queries, keys, values, context, middle, one, second, gate, row, lse = run_attention(
        info, tokens, came, vectors, weights
    )

    first, *others = bits_of("dp")
    crossed = others[::-1]
    own = bit_of(first)
    mine = jnp.stack([me, own])
    far = [move_far(d) for d in distances]

    seq_bits = bits_of("seq")
    pair = lambda n: (others[n], crossed[n])
    core = lambda sent, kept: Stage([sent], [move_by(first)], lambda came: [add_low(kept, came[0])])
    join = lambda fields: [jnp.concatenate(fields)]

    *mixed, back_sum, grad_middle, grad_one, grad_logit, sums, down_send, down_keep, up_send, up_keep, bias_grad = (
        run_feed(
            after(mine, *grad_came[1:]),
            flat(second),
            flat(row),
            up_weight,
            up_bias[None].astype(F32),
            down_weight,
            flat(middle),
            flat(one),
            flat(gate),
            vectors,
            images,
            grad_came,
        )
    )
    (gated,), pending = begin(
        [Stage([down_send, up_send], [move_by(first)] * 2, lambda came: came)], info
    )
    feed_came, came = end(pending)
    feed = [add_low(down_keep, feed_came[0]), add_low(up_keep, feed_came[1])]
    (gated,), pending = begin([scatter_stage(feed, pair(0))], after(gated, *came))
    mixed_came = [
        begin([Stage([after(part, gated)], [move], list)])[1] for part, move in zip(mixed[1:], far)
    ]

    fields = (
        x,
        queries,
        keys,
        values,
        lse,
        cube(grad_one),
        cube(grad_middle),
        cube(grad_logit),
        normed,
    )
    tokens_parts = []
    left = [("xy", n) for n in range(1, len(others))] + [("z", s) for s in seq_bits]

    def feed_stage(feed):
        kind, step = left.pop(0)
        if kind == "xy":
            return scatter_stage(feed, pair(step))
        if len(feed) == 2:
            feed = [jnp.concatenate([feed[0], feed[1].reshape(-1, width)])]
        return scatter_stage(feed, [step])

    grads = []
    for image in range(images):
        image_grads, *part, image_sums = run_attention_back(
            image, gated, fields, vectors, weights, parts
        )
        grads.append(image_grads)
        tokens_parts.append(part)
        small = small + image_sums if image else image_sums
        extra = []
        if image < len(mixed_came):
            (mixed_came[image],), extra = end(mixed_came[image], image_sums)
            gated = after(gated, *extra)
        if image == images - 2 or images == 1:
            feed, came = end(pending, image_sums)
            while len(left) > 3:
                (feed,) = exchange(feed_stage(feed))
            (gated,), pending = begin([feed_stage(feed)], after(gated, *came))
    feed, came = end(pending, image_sums)
    joined = lambda m: jnp.concatenate([part[m] for part in tokens_parts])
    tokens_own = [part[0] for part in tokens_parts]
    tokens_came = {0: None}
    near = Stage([joined(1)], far[:1], list)
    (gated,), pending = begin([feed_stage(feed), near], after(mine, *came, *extra))
    four_send, four_keep = run_outer(gated, flat(normed), flat(context), grad_one, grads)
    feed, tokens_came[0], came = end(pending, four_keep[:8])
    mixed_left = images

    small = jnp.concatenate(
        [
            small[:5],
            sums[:3],
            back_sum,
            bias_grad.reshape(-1, width),
        ]
    )
    small_rows = small.shape[0]
    cut = 1 << (len(others) + len(seq_bits))
    small = jnp.pad(small, ((0, -small_rows % cut), (0, 0)))

    def four_parts(came):
        total = add_low(four_keep, came[0])
        half = total.shape[0] // 2
        return [
            jnp.concatenate([total[:half], (small + came[1]).astype(BF16)]),
            total[half:],
        ]

    def feed_back_stage(step, feed):
        kind, step = step
        if kind == "last":
            return feed_stage(feed)
        if kind == "z":
            return gather_stage(feed, [step])
        if len(feed) == 1:
            half = feed[0].shape[0] // 2
            feed = [feed[0][:half], feed[0][half:].reshape(-1, up_keep.shape[1])]
        if kind == "xy":
            return gather_stage(feed, pair(step))
        return Stage(feed, [move_by(first)] * 2, lambda came: list(zip(feed, came)))

    feed_left = [("last", None)] * len(left) + [("z", s) for s in reversed(seq_bits)]
    feed_left += [("xy", n) for n in reversed(range(len(others)))] + [("core", first)]
    four_left = [("core", first)] + [("cut", n) for n in range(len(others))]
    four_left += [("join", s) for s in seq_bits] + [("bind", s) for s in reversed(seq_bits)]
    four_left += [("grow", n) for n in reversed(range(len(others)))]
    count = len(feed_left)
    spans = [(0, 0), (1, 1), (2, 2), (3, 4), (5, 6), (7, 7)]
    if count != len(spans):
        spans = [(n, n) for n in range(count)]
    stages = len(four_left)
    four, feed_pending, widths, came = None, None, None, None
    tokens_spans = [(-1, -1), (5, 6), (3, 4)][: len(far)]
    tokens_spans += [(0, stages)] * (len(far) - len(tokens_spans))
    tokens_pending = {}
    for n, (kind, step) in enumerate(four_left):
        if kind == "core":
            stage = Stage([four_send, small], [move_by(first)] * 2, four_parts)
        elif kind == "cut":
            stage = scatter_stage(four, pair(step))
        elif kind == "join":
            if len(four) == 2:
                widths = four[0].shape[0]
                four = join(four)
            stage = scatter_stage(four, [step])
        elif kind == "bind":
            stage = gather_stage(four, [step])
        else:
            if len(four) == 1:
                four = [four[0][:widths], four[0][widths:]]
            stage = gather_stage(four, pair(step))
        starts = [a for a, _ in spans]
        if n in starts:
            more = feed_back_stage(feed_left[starts.index(n)], feed)
            _, (_, moving) = begin([stage, more])
            count = len(stage.sends)
            pending, feed_pending = ([stage], moving[:count]), ([more], moving[count:])
        else:
            _, pending = begin([stage])
        markers = []
        if n == 1:
            for m in range(mixed_left, len(mixed_came)):
                (mixed_came[m],), _ = end(mixed_came[m])
            mixed = run_place(after(info, *came), [[mixed[0]]] + [[c] for c in mixed_came])
            markers = [mixed]
        if n == stages - 1:
            down, up = (
                run_spread(after(mine, *came), *pair_of, axis) for axis, pair_of in enumerate(feed)
            )
            markers = [down, up]
        for m, (a, b) in enumerate(tokens_spans):
            if a == n and m not in tokens_pending:
                sent = joined(m + 1) if came is None else after(joined(m + 1), *came)
                tokens_pending[m] = begin([Stage([sent], [far[m]], list)])[1]
        four, came = end(pending, *markers)
        for m, (a, b) in enumerate(tokens_spans):
            if b == n:
                tokens_came[m], arrived = end(tokens_pending[m], *came)
                came = came + arrived
        if n in [b for _, b in spans]:
            feed, _ = end(feed_pending, *came)
    small = four[0][-small.shape[0] :].astype(F32)
    four = jnp.concatenate([four[0][: -small.shape[0]], four[1]])
    _, pending = begin([Stage([four], [move_by(first)], lambda came: came)])
    for m in range(len(far)):
        if m not in tokens_came:
            tokens_came[m], _ = end(tokens_pending[m], *came)
    tokens_grad = run_place(
        after(info, *came), [tokens_own] + [[tokens_came[m][0]] for m in range(len(far))]
    )
    (four_other,), _ = end(pending, tokens_grad)
    four = run_split(mine, four, four_other)
    return (
        mixed,
        tokens_grad,
        four[0],
        small[0],
        four[1],
        four[2],
        small[1],
        four[3],
        small[7],
        up,
        small[9:small_rows].reshape(-1),
        down,
        small[8],
        small[2],
        small[3],
        small[5],
        small[6],
        small[4],
    )


def solution(mesh):
    rows = P("dp", "seq", None)
    in_specs = (rows, P("dp"), rows) + (P(),) * 16
    out_specs = (rows, rows) + (P(),) * 16
    return jax.shard_map(
        on_device, mesh=mesh, in_specs=in_specs, out_specs=out_specs, check_vma=False
    )
```

profile of v0, /device:TPU:0, one launch (start us, length us, event | category | flops | bytes accessed | tf_op | source)
XLA Modules:
  0.0 362.2 jit_solution(17574589667812690986)
XLA Ops:
  0.8 2.3 constant_dynamic-slice_fusion.9
  3.1 4.0 %collective-permute-start.5 = (bf16[3,80,768]{2,1,0:T(8,128)(2,1)}, bf16[3,80,768]{2,1,0:T(8,128)(2,1)S(1)}, u32[]{:S(2)}, u32[]{:S(2)}) collective-permute-start(bf16[3,80,768]{2,1,0:T(8,128)(2,1)} %get-tuple-element.295), channel_id=1, source_target_pairs={{0,2},{1,3},{2,0},{3,1},{4,6},{5,7},{6,4},{7,5},{8,10},{9,11},{10,... | collective-permute-start | bytes 1105928 | tf_op jit(solution)/shard_map/ppermute | solution.py:594
  7.2 1.6 collective-permute-start.4
  9.4 23.7 %collective-permute-done.refs_3_ = bf16[3,80,768]{2,1,0:T(8,128)(2,1)} collective-permute-done((bf16[3,80,768]{2,1,0:T(8,128)(2,1)}, bf16[3,80,768]{2,1,0:T(8,128)(2,1)}, u32[]{:S(2)}, u32[]{:S(2)}) %collective-permute-start) | collective-permute-done | bytes 368672 | tf_op jit(solution)/shard_map/ppermute | solution.py:594
  33.1 7.4 %collective-permute-start.1 = (bf16[3,80,768]{2,1,0:T(8,128)(2,1)S(1)}, bf16[3,80,768]{2,1,0:T(8,128)(2,1)S(1)}, u32[]{:S(2)}, u32[]{:S(2)}) collective-permute-start(bf16[3,80,768]{2,1,0:T(8,128)(2,1)S(1)} %get-tuple-element.151), channel_id=1, source_target_pairs={{0,1},{1,0},{2,3},{3,2},{4,5},{5,4},{6,7},{7,6},{8,9},{9,8},{10,11... | collective-permute-start | bytes 1105928 | tf_op jit(solution)/shard_map/ppermute | solution.py:594
  40.5 1.9 collective-permute-start.2
  42.4 1.5 collective-permute-start.3
  45.2 1.3 copy-done.5
  46.4 1.3 copy-done.7
  49.0 18.0 %attention_forward.1 = (bf16[3,320,768]{2,1,0:T(8,128)(2,1)S(1)}, bf16[3,320,768]{2,1,0:T(8,128)(2,1)S(1)}, bf16[3,320,768]{2,1,0:T(8,128)(2,1)S(1)}, bf16[3,320...) custom-call(s32[4]{0:T(128)S(1)} %pad_add_fusion.info, ...), custom_call_target="tpu_custom_call" | custom-call | flops 23000000512 | bytes 1000000 | tf_op jit(solution)/shard_map/attention_forward/pallas_call | solution.py:150
  67.0 1.6 copy-done.15
  76.1 43.2 %feed.1 = (bf16[3,80,768]{2,1,0:T(8,128)(2,1)S(1)}, bf16[3,80,768]{2,1,0:T(8,128)(2,1)}, bf16[3,80,768]{2,1,0:T(8,128)(2,1)}, bf16[3,80,768]{2,1,0:T(8,128)(2,1)...) custom-call(s32[2]{0:T(128)S(1)} %pad_add_fusion.1.info, ...), custom_call_target="tpu_custom_call" | custom-call | flops 49450000384 | bytes 1000000 | tf_op jit(solution)/shard_map/feed/pallas_call | solution.py:273
  124.1 3.1 collective-permute-done.6
  127.3 3.4 collective-permute-done.7
  130.7 2.4 add_convert_fusion.2
  133.1 2.6 add_convert_fusion.1
  136.6 2.4 collective-permute-start.9
  139.0 1.5 collective-permute-start.14
  140.5 1.5 collective-permute-start.10
  142.0 1.5 collective-permute-start.11
  143.6 8.8 %attention_backward.3 = (bf16[3,320,768]{2,1,0:T(8,128)(2,1)S(1)}, bf16[1,80,768]{2,1,0:T(8,128)(2,1)S(1)}, bf16[1,80,768]{2,1,0:T(8,128)(2,1)S(1)}, bf16[1,80,7...) custom-call(s32[4]{0:T(128)S(1)} %pad_add_fusion.info, ...), custom_call_target="tpu_custom_call" | custom-call | flops 12650000384 | bytes 1000000 | tf_op jit(solution)/shard_map/attention_backward/pallas_call | solution.py:393
  152.4 2.0 collective-permute-done.8.refs_1_
  154.4 9.0 %attention_backward.4 = (bf16[3,320,768]{2,1,0:T(8,128)(2,1)S(1)}, bf16[1,80,768]{2,1,0:T(8,128)(2,1)S(1)}, bf16[1,80,768]{2,1,0:T(8,128)(2,1)S(1)}, bf16[1,80,7...) custom-call(s32[4]{0:T(128)S(1)} %pad_add_fusion.info, ...), custom_call_target="tpu_custom_call" | custom-call | flops 12650000384 | bytes 1000000 | tf_op jit(solution)/shard_map/attention_backward/pallas_call | solution.py:393
  163.5 1.6 collective-permute-done.9.refs_2_
  165.0 2.6 collective-permute-done.10
  169.6 1.6 collective-permute-start.12
  171.7 9.0 %attention_backward.5 = (bf16[3,320,768]{2,1,0:T(8,128)(2,1)S(1)}, bf16[1,80,768]{2,1,0:T(8,128)(2,1)S(1)}, bf16[1,80,768]{2,1,0:T(8,128)(2,1)S(1)}, bf16[1,80,7...) custom-call(s32[4]{0:T(128)S(1)} %pad_add_fusion.info, ...), custom_call_target="tpu_custom_call" | custom-call | flops 12650000384 | bytes 1000000 | tf_op jit(solution)/shard_map/attention_backward/pallas_call | solution.py:393
  186.3 1.8 collective-permute-start.15
  188.1 1.4 copy-done.20
  189.5 1.4 copy-done.23
  190.8 1.4 copy-done.31
  192.2 1.4 copy-done.33
  193.6 1.4 copy-done.35
  195.0 8.1 %outer.1 = (bf16[1536,768]{1,0:T(8,128)(2,1)}, bf16[1536,768]{1,0:T(8,128)(2,1)S(1)}) custom-call(s32[2]{0:T(128)S(1)} %pad_add_fusion.1.info, bf16[960,768]{1,0:T(8,128)(2,1)S(1)} %bitcast.15, bf16[960,768]{1,0:T(8,128)(2,1)S(1)} %bitcast.16, bf16[960,768]{1,0:T(8,128)(2,1)S(1)} %copy-done.23, bf16[3,320,768]{2,1,0:T(8,128)(2,1)S(1)} %copy-done.31, ...), custom_call_target="tpu_custom_call" | custom-call | flops 10350000128 | bytes 1000000 | tf_op jit(solution)/shard_map/outer/pallas_call | solution.py:444
  203.1 3.2 collective-permute-done.15
  210.3 3.3 collective-permute-done.18
  214.4 2.3 add_convert_fusion
  216.9 8.6 %collective-permute-done.19 = bf16[192,768]{1,0:T(8,128)(2,1)S(1)} collective-permute-done((bf16[192,768]{1,0:T(8,128)(2,1)}, bf16[192,768]{1,0:T(8,128)(2,1)S(1)}, u32[]{:S(2)}, u32[]{:S(2)}) %collective-permute-start.19) | collective-permute-done | bytes 294944 | tf_op jit(solution)/shard_map/ppermute | solution.py:489
  229.5 2.5 place.2
  231.9 12.2 %collective-permute-done.21 = bf16[384,768]{1,0:T(8,128)(2,1)} collective-permute-done((bf16[384,768]{1,0:T(8,128)(2,1)}, bf16[384,768]{1,0:T(8,128)(2,1)}, u32[]{:S(2)}, u32[]{:S(2)}) %collective-permute-start.21) | collective-permute-done | bytes 589856 | tf_op jit(solution)/shard_map/ppermute | solution.py:489
  245.4 1.7 add_convert_fusion.5
  248.7 1.4 collective-permute-start.24
  250.1 6.3 %collective-permute-done.24 = bf16[192,768]{1,0:T(8,128)(2,1)S(1)} collective-permute-done((bf16[192,768]{1,0:T(8,128)(2,1)S(1)}, bf16[192,768]{1,0:T(8,128)(2,1)S(1)}, u32[]{:S(2)}, u32[]{:S(2)}) %collective-permute-start.24) | collective-permute-done | bytes 294944 | tf_op jit(solution)/shard_map/ppermute | solution.py:489
  258.1 5.5 %collective-permute-done.25 = bf16[384,768]{1,0:T(8,128)(2,1)S(1)} collective-permute-done((bf16[384,768]{1,0:T(8,128)(2,1)S(1)}, bf16[384,768]{1,0:T(8,128)(2,1)S(1)}, u32[]{:S(2)}, u32[]{:S(2)}) %collective-permute-start.25) | collective-permute-done | bytes 589856 | tf_op jit(solution)/shard_map/ppermute | solution.py:489
  265.0 1.3 reshape.96
  266.6 2.2 collective-permute-start.30
  268.8 1.5 collective-permute-start.28
  271.1 7.4 %collective-permute-done.26 = bf16[194,768]{1,0:T(8,128)(2,1)} collective-permute-done((bf16[194,768]{1,0:T(8,128)(2,1)S(1)}, bf16[194,768]{1,0:T(8,128)(2,1)}, u32[]{:S(2)}, u32[]{:S(2)}) %collective-permute-start.26) | collective-permute-done | bytes 298016 | tf_op jit(solution)/shard_map/ppermute | solution.py:489
  278.5 1.4 add_convert_fusion.10
  280.1 10.2 %collective-permute-done.27 = bf16[97,768]{1,0:T(8,128)(2,1)S(1)} collective-permute-done((bf16[97,768]{1,0:T(8,128)(2,1)S(1)}, bf16[97,768]{1,0:T(8,128)(2,1)S(1)}, u32[]{:S(2)}, u32[]{:S(2)}) %collective-permute-start.27) | collective-permute-done | bytes 149024 | tf_op jit(solution)/shard_map/ppermute | solution.py:489
  290.4 1.6 maximum_select_fusion.4
  292.1 1.7 maximum_select_fusion.5
  294.9 1.5 collective-permute-start.34
  296.4 8.0 %collective-permute-done.31 = bf16[97,768]{1,0:T(8,128)(2,1)S(1)} collective-permute-done((bf16[97,768]{1,0:T(8,128)(2,1)S(1)}, bf16[97,768]{1,0:T(8,128)(2,1)S(1)}, u32[]{:S(2)}, u32[]{:S(2)}) %collective-permute-start.31) | collective-permute-done | bytes 149024 | tf_op jit(solution)/shard_map/ppermute | solution.py:489
  304.6 2.3 collective-permute-start.35
  306.9 7.9 %collective-permute-done.32 = bf16[194,768]{1,0:T(8,128)(2,1)S(1)} collective-permute-done((bf16[194,768]{1,0:T(8,128)(2,1)S(1)}, bf16[194,768]{1,0:T(8,128)(2,1)S(1)}, u32[]{:S(2)}, u32[]{:S(2)}) %collective-permute-start.32) | collective-permute-done | bytes 298016 | tf_op jit(solution)/shard_map/ppermute | solution.py:489
  315.1 4.3 %collective-permute-done.35.refs_4_ = bf16[3,80,768]{2,1,0:T(8,128)(2,1)S(1)} collective-permute-done((bf16[3,80,768]{2,1,0:T(8,128)(2,1)S(1)}, bf16[3,80,768]{2,1,0:T(8,128)(2,1)S(1)}, u32[]{:S(2)}, u32[]{:S(2)}) %collective-permute-start.35) | collective-permute-done | bytes 368672 | tf_op jit(solution)/shard_map/ppermute | solution.py:594
  321.4 1.4 collective-permute-start.36
  323.5 7.9 %collective-permute-done.37 = bf16[192,768]{1,0:T(8,128)(2,1)S(1)} collective-permute-done((bf16[192,768]{1,0:T(8,128)(2,1)S(1)}, bf16[192,768]{1,0:T(8,128)(2,1)S(1)}, u32[]{:S(2)}, u32[]{:S(2)}) %collective-permute-start.37) | collective-permute-done | bytes 294944 | tf_op jit(solution)/shard_map/ppermute | solution.py:489
  333.5 4.5 %spread.2 = f32[3072,768]{1,0:T(8,128)} custom-call(s32[2]{0:T(128)S(1)} %pad_add_fusion.1.info, bf16[1536,768]{1,0:T(8,128)(2,1)S(1)} %maximum_select_fusion.own, bf16[1536,768]{1,0:T(8,128)(2,1)S(1)} %collective-permute-done.40.other), custom_call_target="tpu_custom_call" | custom-call | flops 8049999872 | bytes 1000000 | tf_op jit(solution)/shard_map/spread/pallas_call | solution.py:529
  338.0 4.5 %spread.3 = f32[768,3072]{1,0:T(8,128)} custom-call(s32[2]{0:T(128)S(1)} %pad_add_fusion.1.info, bf16[768,1536]{1,0:T(8,128)(2,1)S(1)} %maximum_select_fusion.1.own, bf16[768,1536]{1,0:T(8,128)(2,1)S(1)} %collective-permute-done.41.other), custom_call_target="tpu_custom_call" | custom-call | flops 8049999872 | bytes 1000000 | tf_op jit(solution)/shard_map/spread/pallas_call | solution.py:529
  342.5 3.6 collective-permute-done.39
  352.2 2.2 place.3
  354.4 7.4 %split.1 = (f32[768,768]{1,0:T(8,128)}, f32[768,768]{1,0:T(8,128)}, f32[768,768]{1,0:T(8,128)}, f32[768,768]{1,0:T(8,128)}) custom-call(s32[2]{0:T(128)S(1)} %pad_add_fusion.1.info, bf16[1536,768]{1,0:T(8,128)(2,1)S(1)} %pad_maximum_fusion.own, bf16[1536,768]{1,0:T(8,128)(2,1)} %collective-permute-done.42.other), custom_call_target="tpu_custom_call" | custom-call | flops 9200000000 | bytes 1000000 | tf_op jit(solution)/shard_map/split/pallas_call | solution.py:570
  (270 shorter events, 52.8 us)
Async XLA Ops:
  3.1 40.8 %collective-permute-start.5 = (bf16[3,80,768]{2,1,0:T(8,128)(2,1)}, bf16[3,80,768]{2,1,0:T(8,128)(2,1)S(1)}, u32[]{:S(2)}, u32[]{:S(2)}) collective-permute-start(bf16[3,80,768]{2,1,0:T(8,128)(2,1)} %get-tuple-element.295), channel_id=1, source_target_pairs={{0,2},{1,3},{2,0},{3,1},{4,6},{5,7},{6,4},{7,5},{8,10},{9,11},{10,... | collective-permute-start | bytes 1105928 | tf_op jit(solution)/shard_map/ppermute | solution.py:594
  7.2 36.7 %collective-permute-start.4 = (bf16[3,80,768]{2,1,0:T(8,128)(2,1)}, bf16[3,80,768]{2,1,0:T(8,128)(2,1)}, u32[]{:S(2)}, u32[]{:S(2)}) collective-permute-start(bf16[3,80,768]{2,1,0:T(8,128)(2,1)} %get-tuple-element.296), channel_id=1, source_target_pairs={{0,1},{1,0},{2,3},{3,2},{4,5},{5,4},{6,7},{7,6},{8,9},{9,8},{10,11... | collective-permute-start | bytes 1105928 | tf_op jit(solution)/shard_map/ppermute | solution.py:594
  8.8 24.3 %collective-permute-start = (bf16[3,80,768]{2,1,0:T(8,128)(2,1)}, bf16[3,80,768]{2,1,0:T(8,128)(2,1)}, u32[]{:S(2)}, u32[]{:S(2)}) collective-permute-start(bf16[3,80,768]{2,1,0:T(8,128)(2,1)} %get-tuple-element.297), channel_id=1, source_target_pairs={{0,3},{1,2},{2,1},{3,0},{4,7},{5,6},{6,5},{7,4},{8,11},{9,10},{10,... | collective-permute-start | bytes 1105928 | tf_op jit(solution)/shard_map/ppermute | solution.py:594
  8.9 35.0 %copy-start = (bf16[12,80,768]{2,1,0:T(8,128)(2,1)S(1)}, bf16[12,80,768]{2,1,0:T(8,128)(2,1)}, u32[]{:S(2)}) copy-start(bf16[12,80,768]{2,1,0:T(8,128)(2,1)} %refs_0_.2) | copy-start | bytes 4423684
  33.1 43.0 %copy-start.2 = (bf16[12,80,768]{2,1,0:T(8,128)(2,1)S(1)}, bf16[12,80,768]{2,1,0:T(8,128)(2,1)}, u32[]{:S(2)}) copy-start(bf16[12,80,768]{2,1,0:T(8,128)(2,1)} %refs_0_.3) | copy-start | bytes 4423684
  33.1 43.0 %collective-permute-start.1 = (bf16[3,80,768]{2,1,0:T(8,128)(2,1)S(1)}, bf16[3,80,768]{2,1,0:T(8,128)(2,1)S(1)}, u32[]{:S(2)}, u32[]{:S(2)}) collective-permute-start(bf16[3,80,768]{2,1,0:T(8,128)(2,1)S(1)} %get-tuple-element.151), channel_id=1, source_target_pairs={{0,1},{1,0},{2,3},{3,2},{4,5},{5,4},{6,7},{7,6},{8,9},{9,8},{10,11... | collective-permute-start | bytes 1105928 | tf_op jit(solution)/shard_map/ppermute | solution.py:594
  40.5 35.6 %collective-permute-start.2 = (bf16[3,80,768]{2,1,0:T(8,128)(2,1)S(1)}, bf16[3,80,768]{2,1,0:T(8,128)(2,1)S(1)}, u32[]{:S(2)}, u32[]{:S(2)}) collective-permute-start(bf16[3,80,768]{2,1,0:T(8,128)(2,1)S(1)} %get-tuple-element.152), channel_id=1, source_target_pairs={{0,2},{1,3},{2,0},{3,1},{4,6},{5,7},{6,4},{7,5},{8,10},{9,11},{10,... | collective-permute-start | bytes 1105928 | tf_op jit(solution)/shard_map/ppermute | solution.py:594
  42.4 33.7 %collective-permute-start.3 = (bf16[3,80,768]{2,1,0:T(8,128)(2,1)S(1)}, bf16[3,80,768]{2,1,0:T(8,128)(2,1)S(1)}, u32[]{:S(2)}, u32[]{:S(2)}) collective-permute-start(bf16[3,80,768]{2,1,0:T(8,128)(2,1)S(1)} %get-tuple-element.153), channel_id=1, source_target_pairs={{0,3},{1,2},{2,1},{3,0},{4,7},{5,6},{6,5},{7,4},{8,11},{9,10},{10,... | collective-permute-start | bytes 1105928 | tf_op jit(solution)/shard_map/ppermute | solution.py:594
  122.4 10.7 %copy-start.28 = (bf16[3,80,768]{2,1,0:T(8,128)(2,1)}, bf16[3,80,768]{2,1,0:T(8,128)(2,1)S(1)}, u32[]{:S(2)}) copy-start(bf16[3,80,768]{2,1,0:T(8,128)(2,1)S(1)} %get-tuple-element.225.refs_0_) | copy-start | bytes 1105924
  122.4 4.9 %collective-permute-start.6 = (bf16[1536,768]{1,0:T(8,128)(2,1)}, bf16[1536,768]{1,0:T(8,128)(2,1)}, u32[]{:S(2)}, u32[]{:S(2)}) collective-permute-start(bf16[1536,768]{1,0:T(8,128)(2,1)} %get-tuple-element.163), channel_id=1, source_target_pairs={{0,4},{4,0},{8,12},{12,8},{16,20},{20,16},{24,28},{28,24},{1,5},{5... | collective-permute-start | bytes 7077896 | tf_op jit(solution)/shard_map/ppermute | solution.py:489
  122.4 8.2 %collective-permute-start.7 = (bf16[768,1536]{1,0:T(8,128)(2,1)}, bf16[768,1536]{1,0:T(8,128)(2,1)}, u32[]{:S(2)}, u32[]{:S(2)}) collective-permute-start(bf16[768,1536]{1,0:T(8,128)(2,1)} %get-tuple-element.164), channel_id=1, source_target_pairs={{0,4},{4,0},{8,12},{12,8},{16,20},{20,16},{24,28},{28,24},{1,5},{5... | collective-permute-start | bytes 7077896 | tf_op jit(solution)/shard_map/ppermute | solution.py:489
  124.1 56.7 %copy-start.65 = (f32[4,768]{1,0:T(4,128)}, f32[4,768]{1,0:T(4,128)S(1)}, u32[]{:S(2)}) copy-start(f32[4,768]{1,0:T(4,128)S(1)} %reshape.95) | copy-start | bytes 36868
  124.1 56.7 %copy-start.67 = (f32[3,768]{1,0:T(4,128)}, f32[3,768]{1,0:T(4,128)S(1)}, u32[]{:S(2)}) copy-start(f32[3,768]{1,0:T(4,128)S(1)} %slice.62) | copy-start | bytes 27652
  130.6 12.8 %copy-start.39 = (bf16[3,320,768]{2,1,0:T(8,128)(2,1)S(1)}, bf16[3,320,768]{2,1,0:T(8,128)(2,1)}, u32[]{:S(2)}) copy-start(bf16[3,320,768]{2,1,0:T(8,128)(2,1)} %copy-done.38) | copy-start | bytes 4423684
  130.7 12.8 %copy-start.41 = (bf16[3,320,768]{2,1,0:T(8,128)(2,1)S(1)}, bf16[3,320,768]{2,1,0:T(8,128)(2,1)}, u32[]{:S(2)}) copy-start(bf16[3,320,768]{2,1,0:T(8,128)(2,1)} %copy-done.40) | copy-start | bytes 4423684
  130.7 12.8 %copy-start.43 = (bf16[3,320,768]{2,1,0:T(8,128)(2,1)S(1)}, bf16[3,320,768]{2,1,0:T(8,128)(2,1)}, u32[]{:S(2)}) copy-start(bf16[3,320,768]{2,1,0:T(8,128)(2,1)} %copy-done.42) | copy-start | bytes 4423684
  133.1 10.4 %copy-start.17 = (bf16[3,320,768]{2,1,0:T(8,128)(2,1)S(1)}, bf16[3,320,768]{2,1,0:T(8,128)(2,1)}, u32[]{:S(2)}) copy-start(bf16[3,320,768]{2,1,0:T(8,128)(2,1)} %copy-done.16) | copy-start | bytes 4423684
  133.1 10.4 %copy-start.22 = (bf16[960,768]{1,0:T(8,128)(2,1)S(1)}, bf16[960,768]{1,0:T(8,128)(2,1)}, u32[]{:S(2)}) copy-start(bf16[960,768]{1,0:T(8,128)(2,1)} %copy-done.21) | copy-start | bytes 4423684
  133.1 10.4 %copy-start.25 = (bf16[960,768]{1,0:T(8,128)(2,1)S(1)}, bf16[960,768]{1,0:T(8,128)(2,1)}, u32[]{:S(2)}) copy-start(bf16[960,768]{1,0:T(8,128)(2,1)} %copy-done.24) | copy-start | bytes 4423684
  133.1 10.4 %copy-start.27 = (f32[960,128]{1,0:T(8,128)S(1)}, f32[960,128]{1,0:T(8,128)}, u32[]{:S(2)}) copy-start(f32[960,128]{1,0:T(8,128)} %copy-done.26) | copy-start | bytes 1474564
  133.1 10.4 %copy-start.37 = (bf16[3,320,768]{2,1,0:T(8,128)(2,1)S(1)}, bf16[3,320,768]{2,1,0:T(8,128)(2,1)}, u32[]{:S(2)}) copy-start(bf16[3,320,768]{2,1,0:T(8,128)(2,1)} %copy-done.36) | copy-start | bytes 4423684
  136.0 18.4 %collective-permute-start.8 = (bf16[3,80,768]{2,1,0:T(8,128)(2,1)}, bf16[3,80,768]{2,1,0:T(8,128)(2,1)S(1)}, u32[]{:S(2)}, u32[]{:S(2)}) collective-permute-start(bf16[3,80,768]{2,1,0:T(8,128)(2,1)} %get-tuple-element.172), channel_id=1, source_target_pairs={{0,1},{1,0},{2,3},{3,2},{4,5},{5,4},{6,7},{7,6},{8,9},{9,8},{10,11... | collective-permute-start | bytes 1105928 | tf_op jit(solution)/shard_map/ppermute | solution.py:594
  136.6 28.4 %collective-permute-start.9 = (bf16[3,80,768]{2,1,0:T(8,128)(2,1)}, bf16[3,80,768]{2,1,0:T(8,128)(2,1)S(1)}, u32[]{:S(2)}, u32[]{:S(2)}) collective-permute-start(bf16[3,80,768]{2,1,0:T(8,128)(2,1)} %get-tuple-element.186), channel_id=1, source_target_pairs={{0,2},{1,3},{2,0},{3,1},{4,6},{5,7},{6,4},{7,5},{8,10},{9,11},{10,... | collective-permute-start | bytes 1105928 | tf_op jit(solution)/shard_map/ppermute | solution.py:594
  139.0 41.8 %collective-permute-start.14 = (bf16[3,80,768]{2,1,0:T(8,128)(2,1)}, bf16[3,80,768]{2,1,0:T(8,128)(2,1)S(1)}, u32[]{:S(2)}, u32[]{:S(2)}) collective-permute-start(bf16[3,80,768]{2,1,0:T(8,128)(2,1)} %get-tuple-element.202), channel_id=1, source_target_pairs={{0,3},{1,2},{2,1},{3,0},{4,7},{5,6},{6,5},{7,4},{8,11},{9,10},{10,... | collective-permute-start | bytes 1105928 | tf_op jit(solution)/shard_map/ppermute | solution.py:594
  140.5 27.2 %collective-permute-start.10 = (bf16[768,768]{1,0:T(8,128)(2,1)S(1)}, bf16[768,768]{1,0:T(8,128)(2,1)S(1)}, u32[]{:S(2)}, u32[]{:S(2)}) collective-permute-start(bf16[768,768]{1,0:T(8,128)(2,1)S(1)} %constant_dynamic-slice_fusion.8), channel_id=1, source_target_pairs={{0,8},{4,12},{8,0},{12,4},{16,24},{20,28},{24,16},{28,20},{1,9},{5... | collective-permute-start | bytes 3538952 | tf_op jit(solution)/shard_map/ppermute | solution.py:489
  142.0 26.9 %collective-permute-start.11 = (bf16[384,1536]{1,0:T(8,128)(2,1)S(1)}, bf16[384,1536]{1,0:T(8,128)(2,1)S(1)}, u32[]{:S(2)}, u32[]{:S(2)}) collective-permute-start(bf16[384,1536]{1,0:T(8,128)(2,1)S(1)} %constant_dynamic-slice_fusion.7), channel_id=1, source_target_pairs={{0,16},{4,20},{8,24},{12,28},{16,0},{20,4},{24,8},{28,12},{1,17},{... | collective-permute-start | bytes 3538952 | tf_op jit(solution)/shard_map/ppermute | solution.py:489
  152.4 11.0 %copy-start.30 = (bf16[3,320,768]{2,1,0:T(8,128)(2,1)}, bf16[3,320,768]{2,1,0:T(8,128)(2,1)S(1)}, u32[]{:S(2)}) copy-start(bf16[3,320,768]{2,1,0:T(8,128)(2,1)S(1)} %get-tuple-element.210.refs_0_) | copy-start | bytes 4423684
  152.4 11.0 %copy-start.44 = (bf16[1,80,768]{2,1,0:T(8,128)(2,1)}, bf16[1,80,768]{2,1,0:T(8,128)(2,1)S(1)}, u32[]{:S(2)}) copy-start(bf16[1,80,768]{2,1,0:T(8,128)(2,1)S(1)} %get-tuple-element.275.refs_0_) | copy-start | bytes 368644
  169.6 13.4 %collective-permute-start.12 = (bf16[384,768]{1,0:T(8,128)(2,1)S(1)}, bf16[384,768]{1,0:T(8,128)(2,1)S(1)}, u32[]{:S(2)}, u32[]{:S(2)}) collective-permute-start(bf16[384,768]{1,0:T(8,128)(2,1)S(1)} %constant_dynamic-slice_fusion.6), channel_id=1, source_target_pairs={{0,16},{4,20},{8,24},{12,28},{16,0},{20,4},{24,8},{28,12},{1,17},{... | collective-permute-start | bytes 1769480 | tf_op jit(solution)/shard_map/ppermute | solution.py:489
  171.2 13.0 %collective-permute-start.13 = (bf16[192,1536]{1,0:T(8,128)(2,1)S(1)}, bf16[192,1536]{1,0:T(8,128)(2,1)S(1)}, u32[]{:S(2)}, u32[]{:S(2)}) collective-permute-start(bf16[192,1536]{1,0:T(8,128)(2,1)S(1)} %constant_dynamic-slice_fusion.5), channel_id=1, source_target_pairs={{0,8},{4,12},{8,0},{12,4},{16,24},{20,28},{24,16},{28,20},{1,9},{5... | collective-permute-start | bytes 1769480 | tf_op jit(solution)/shard_map/ppermute | solution.py:489
  186.0 17.1 %collective-permute-start.16 = (bf16[3,80,768]{2,1,0:T(8,128)(2,1)}, bf16[3,80,768]{2,1,0:T(8,128)(2,1)S(1)}, u32[]{:S(2)}, u32[]{:S(2)}) collective-permute-start(bf16[3,80,768]{2,1,0:T(8,128)(2,1)} %get-tuple-element.218), channel_id=1, source_target_pairs={{0,1},{1,0},{2,3},{3,2},{4,5},{5,4},{6,7},{7,6},{8,9},{9,8},{10,11... | collective-permute-start | bytes 1105928 | tf_op jit(solution)/shard_map/ppermute | solution.py:594
  186.3 20.0 %collective-permute-start.15 = (bf16[384,768]{1,0:T(8,128)(2,1)S(1)}, bf16[384,768]{1,0:T(8,128)(2,1)S(1)}, u32[]{:S(2)}, u32[]{:S(2)}) collective-permute-start(bf16[384,768]{1,0:T(8,128)(2,1)S(1)} %fusion.3), channel_id=1, source_target_pairs={{0,1},{1,0},{2,3},{3,2},{4,5},{5,4},{6,7},{7,6},{8,9},{9,8},{10,11... | collective-permute-start | bytes 1769480 | tf_op jit(solution)/shard_map/ppermute | solution.py:489
  195.0 11.3 %copy-start.53 = (bf16[384,768]{1,0:T(8,128)(2,1)S(1)}, bf16[384,768]{1,0:T(8,128)(2,1)}, u32[]{:S(2)}) copy-start(bf16[384,768]{1,0:T(8,128)(2,1)} %copy-done.52) | copy-start | bytes 1769476
  195.0 11.3 %copy-start.55 = (bf16[384,768]{1,0:T(8,128)(2,1)S(1)}, bf16[384,768]{1,0:T(8,128)(2,1)}, u32[]{:S(2)}) copy-start(bf16[384,768]{1,0:T(8,128)(2,1)} %copy-done.54) | copy-start | bytes 1769476
  203.1 10.5 %copy-start.66 = (f32[4,768]{1,0:T(4,128)S(1)}, f32[4,768]{1,0:T(4,128)}, u32[]{:S(2)}) copy-start(f32[4,768]{1,0:T(4,128)} %copy-done.65) | copy-start | bytes 36868
  203.1 10.5 %copy-start.68 = (f32[3,768]{1,0:T(4,128)S(1)}, f32[3,768]{1,0:T(4,128)}, u32[]{:S(2)}) copy-start(f32[3,768]{1,0:T(4,128)} %copy-done.67) | copy-start | bytes 27652
  208.6 5.0 %collective-permute-start.17 = (bf16[1536,768]{1,0:T(8,128)(2,1)}, bf16[1536,768]{1,0:T(8,128)(2,1)}, u32[]{:S(2)}, u32[]{:S(2)}) collective-permute-start(bf16[1536,768]{1,0:T(8,128)(2,1)} %get-tuple-element.220), channel_id=1, source_target_pairs={{0,4},{4,0},{8,12},{12,8},{16,20},{20,16},{24,28},{28,24},{1,5},{5... | collective-permute-start | bytes 7077896 | tf_op jit(solution)/shard_map/ppermute | solution.py:489
  208.6 4.9 %collective-permute-start.18 = (f32[16,768]{1,0:T(8,128)}, f32[16,768]{1,0:T(8,128)}, u32[]{:S(2)}, u32[]{:S(2)}) collective-permute-start(f32[16,768]{1,0:T(8,128)} %select_maximum_fusion), channel_id=1, source_target_pairs={{0,4},{4,0},{8,12},{12,8},{16,20},{20,16},{24,28},{28,24},{1,5},{5... | collective-permute-start | bytes 147464 | tf_op jit(solution)/shard_map/ppermute | solution.py:489
  209.1 16.3 %collective-permute-start.19 = (bf16[192,768]{1,0:T(8,128)(2,1)}, bf16[192,768]{1,0:T(8,128)(2,1)S(1)}, u32[]{:S(2)}, u32[]{:S(2)}) collective-permute-start(bf16[192,768]{1,0:T(8,128)(2,1)} %constant_dynamic-slice_fusion.4), channel_id=1, source_target_pairs={{0,2},{1,3},{2,0},{3,1},{4,6},{5,7},{6,4},{7,5},{8,10},{9,11},{10,... | collective-permute-start | bytes 884744 | tf_op jit(solution)/shard_map/ppermute | solution.py:489
  216.8 11.4 %copy-start.56 = (bf16[768,768]{1,0:T(8,128)(2,1)}, bf16[768,768]{1,0:T(8,128)(2,1)S(1)}, u32[]{:S(2)}) copy-start(bf16[768,768]{1,0:T(8,128)(2,1)S(1)} %get-tuple-element.293) | copy-start | bytes 3538948
  228.2 15.9 %collective-permute-start.20 = (bf16[392,768]{1,0:T(8,128)(2,1)}, bf16[392,768]{1,0:T(8,128)(2,1)}, u32[]{:S(2)}, u32[]{:S(2)}) collective-permute-start(bf16[392,768]{1,0:T(8,128)(2,1)} %fusion), channel_id=1, source_target_pairs={{0,8},{4,12},{8,0},{12,4},{16,24},{20,28},{24,16},{28,20},{1,9},{5... | collective-permute-start | bytes 1806344 | tf_op jit(solution)/shard_map/ppermute | solution.py:489
  228.9 15.3 %collective-permute-start.21 = (bf16[384,768]{1,0:T(8,128)(2,1)}, bf16[384,768]{1,0:T(8,128)(2,1)}, u32[]{:S(2)}, u32[]{:S(2)}) collective-permute-start(bf16[384,768]{1,0:T(8,128)(2,1)} %constant_dynamic-slice_fusion.3), channel_id=1, source_target_pairs={{0,16},{4,20},{8,24},{12,28},{16,0},{20,4},{24,8},{28,12},{1,17},{... | collective-permute-start | bytes 1769480 | tf_op jit(solution)/shard_map/ppermute | solution.py:489
  229.4 17.7 %collective-permute-start.22 = (bf16[192,768]{1,0:T(8,128)(2,1)}, bf16[192,768]{1,0:T(8,128)(2,1)S(1)}, u32[]{:S(2)}, u32[]{:S(2)}) collective-permute-start(bf16[192,768]{1,0:T(8,128)(2,1)} %add_convert_fusion.13), channel_id=1, source_target_pairs={{0,2},{1,3},{2,0},{3,1},{4,6},{5,7},{6,4},{7,5},{8,10},{9,11},{10,... | collective-permute-start | bytes 884744 | tf_op jit(solution)/shard_map/ppermute | solution.py:489
  229.5 14.7 %copy-start.57 = (bf16[768,768]{1,0:T(8,128)(2,1)S(1)}, bf16[768,768]{1,0:T(8,128)(2,1)}, u32[]{:S(2)}) copy-start(bf16[768,768]{1,0:T(8,128)(2,1)} %copy-done.56) | copy-start | bytes 3538948
  248.0 8.4 %collective-permute-start.23 = (bf16[196,768]{1,0:T(8,128)(2,1)S(1)}, bf16[196,768]{1,0:T(8,128)(2,1)S(1)}, u32[]{:S(2)}, u32[]{:S(2)}) collective-permute-start(bf16[196,768]{1,0:T(8,128)(2,1)S(1)} %constant_dynamic-slice_fusion.2), channel_id=1, source_target_pairs={{0,16},{4,20},{8,24},{12,28},{16,0},{20,4},{24,8},{28,12},{1,17},{... | collective-permute-start | bytes 903176 | tf_op jit(solution)/shard_map/ppermute | solution.py:489
  248.7 7.7 %collective-permute-start.24 = (bf16[192,768]{1,0:T(8,128)(2,1)S(1)}, bf16[192,768]{1,0:T(8,128)(2,1)S(1)}, u32[]{:S(2)}, u32[]{:S(2)}) collective-permute-start(bf16[192,768]{1,0:T(8,128)(2,1)S(1)} %constant_dynamic-slice_fusion.1), channel_id=1, source_target_pairs={{0,8},{4,12},{8,0},{12,4},{16,24},{20,28},{24,16},{28,20},{1,9},{5... | collective-permute-start | bytes 884744 | tf_op jit(solution)/shard_map/ppermute | solution.py:489
  250.1 13.5 %collective-permute-start.25 = (bf16[384,768]{1,0:T(8,128)(2,1)S(1)}, bf16[384,768]{1,0:T(8,128)(2,1)S(1)}, u32[]{:S(2)}, u32[]{:S(2)}) collective-permute-start(bf16[384,768]{1,0:T(8,128)(2,1)S(1)} %maximum_select_fusion.9), channel_id=1, source_target_pairs={{0,1},{1,0},{2,3},{3,2},{4,5},{5,4},{6,7},{7,6},{8,9},{9,8},{10,11... | collective-permute-start | bytes 1769480 | tf_op jit(solution)/shard_map/ppermute | solution.py:489
  266.3 12.3 %collective-permute-start.26 = (bf16[194,768]{1,0:T(8,128)(2,1)S(1)}, bf16[194,768]{1,0:T(8,128)(2,1)}, u32[]{:S(2)}, u32[]{:S(2)}) collective-permute-start(bf16[194,768]{1,0:T(8,128)(2,1)S(1)} %fusion.4), channel_id=1, source_target_pairs={{0,1},{1,0},{2,3},{3,2},{4,5},{5,4},{6,7},{7,6},{8,9},{9,8},{10,11... | collective-permute-start | bytes 893960 | tf_op jit(solution)/shard_map/ppermute | solution.py:489
  266.6 23.7 %collective-permute-start.30 = (bf16[3,80,768]{2,1,0:T(8,128)(2,1)}, bf16[3,80,768]{2,1,0:T(8,128)(2,1)S(1)}, u32[]{:S(2)}, u32[]{:S(2)}) collective-permute-start(bf16[3,80,768]{2,1,0:T(8,128)(2,1)} %get-tuple-element.247), channel_id=1, source_target_pairs={{0,3},{1,2},{2,1},{3,0},{4,7},{5,6},{6,5},{7,4},{8,11},{9,10},{10,... | collective-permute-start | bytes 1105928 | tf_op jit(solution)/shard_map/ppermute | solution.py:594
  268.8 21.6 %collective-permute-start.28 = (bf16[384,768]{1,0:T(8,128)(2,1)S(1)}, bf16[384,768]{1,0:T(8,128)(2,1)}, u32[]{:S(2)}, u32[]{:S(2)}) collective-permute-start(bf16[384,768]{1,0:T(8,128)(2,1)S(1)} %get-tuple-element.242), channel_id=1, source_target_pairs={{0,16},{4,20},{8,24},{12,28},{16,0},{20,4},{24,8},{28,12},{1,17},{... | collective-permute-start | bytes 1769480 | tf_op jit(solution)/shard_map/ppermute | solution.py:489
  270.2 20.2 %collective-permute-start.29 = (bf16[192,1536]{1,0:T(8,128)(2,1)S(1)}, bf16[192,1536]{1,0:T(8,128)(2,1)}, u32[]{:S(2)}, u32[]{:S(2)}) collective-permute-start(bf16[192,1536]{1,0:T(8,128)(2,1)S(1)} %reshape.96), channel_id=1, source_target_pairs={{0,8},{4,12},{8,0},{12,4},{16,24},{20,28},{24,16},{28,20},{1,9},{5... | collective-permute-start | bytes 1769480 | tf_op jit(solution)/shard_map/ppermute | solution.py:489
  280.0 10.3 %collective-permute-start.27 = (bf16[97,768]{1,0:T(8,128)(2,1)S(1)}, bf16[97,768]{1,0:T(8,128)(2,1)S(1)}, u32[]{:S(2)}, u32[]{:S(2)}) collective-permute-start(bf16[97,768]{1,0:T(8,128)(2,1)S(1)} %constant_dynamic-slice_fusion), channel_id=1, source_target_pairs={{0,2},{1,3},{2,0},{3,1},{4,6},{5,7},{6,4},{7,5},{8,10},{9,11},{10,... | collective-permute-start | bytes 446984 | tf_op jit(solution)/shard_map/ppermute | solution.py:489
  293.7 25.7 %collective-permute-start.33 = (bf16[768,768]{1,0:T(8,128)(2,1)S(1)}, bf16[768,768]{1,0:T(8,128)(2,1)S(1)}, u32[]{:S(2)}, u32[]{:S(2)}) collective-permute-start(bf16[768,768]{1,0:T(8,128)(2,1)S(1)} %maximum_select_fusion.4), channel_id=1, source_target_pairs={{0,8},{4,12},{8,0},{12,4},{16,24},{20,28},{24,16},{28,20},{1,9},{5... | collective-permute-start | bytes 3538952 | tf_op jit(solution)/shard_map/ppermute | solution.py:489
  294.9 24.5 %collective-permute-start.34 = (bf16[384,1536]{1,0:T(8,128)(2,1)S(1)}, bf16[384,1536]{1,0:T(8,128)(2,1)S(1)}, u32[]{:S(2)}, u32[]{:S(2)}) collective-permute-start(bf16[384,1536]{1,0:T(8,128)(2,1)S(1)} %maximum_select_fusion.5), channel_id=1, source_target_pairs={{0,16},{4,20},{8,24},{12,28},{16,0},{20,4},{24,8},{28,12},{1,17},{... | collective-permute-start | bytes 3538952 | tf_op jit(solution)/shard_map/ppermute | solution.py:489
  296.4 8.0 %collective-permute-start.31 = (bf16[97,768]{1,0:T(8,128)(2,1)S(1)}, bf16[97,768]{1,0:T(8,128)(2,1)S(1)}, u32[]{:S(2)}, u32[]{:S(2)}) collective-permute-start(bf16[97,768]{1,0:T(8,128)(2,1)S(1)} %add_convert_fusion.14), channel_id=1, source_target_pairs={{0,2},{1,3},{2,0},{3,1},{4,6},{5,7},{6,4},{7,5},{8,10},{9,11},{10,... | collective-permute-start | bytes 446984 | tf_op jit(solution)/shard_map/ppermute | solution.py:489
  304.4 10.4 %collective-permute-start.32 = (bf16[194,768]{1,0:T(8,128)(2,1)S(1)}, bf16[194,768]{1,0:T(8,128)(2,1)S(1)}, u32[]{:S(2)}, u32[]{:S(2)}) collective-permute-start(bf16[194,768]{1,0:T(8,128)(2,1)S(1)} %maximum_select_fusion.11), channel_id=1, source_target_pairs={{0,1},{1,0},{2,3},{3,2},{4,5},{5,4},{6,7},{7,6},{8,9},{9,8},{10,11... | collective-permute-start | bytes 893960 | tf_op jit(solution)/shard_map/ppermute | solution.py:489
  304.6 14.8 %collective-permute-start.35 = (bf16[3,80,768]{2,1,0:T(8,128)(2,1)S(1)}, bf16[3,80,768]{2,1,0:T(8,128)(2,1)S(1)}, u32[]{:S(2)}, u32[]{:S(2)}) collective-permute-start(bf16[3,80,768]{2,1,0:T(8,128)(2,1)S(1)} %pad_maximum_fusion.3), channel_id=1, source_target_pairs={{0,2},{1,3},{2,0},{3,1},{4,6},{5,7},{6,4},{7,5},{8,10},{9,11},{10,... | collective-permute-start | bytes 1105928 | tf_op jit(solution)/shard_map/ppermute | solution.py:594
  320.8 12.7 %collective-permute-start.40 = (bf16[1536,768]{1,0:T(8,128)(2,1)S(1)}, bf16[1536,768]{1,0:T(8,128)(2,1)S(1)}, u32[]{:S(2)}, u32[]{:S(2)}) collective-permute-start(bf16[1536,768]{1,0:T(8,128)(2,1)S(1)} %maximum_select_fusion.own), channel_id=1, source_target_pairs={{0,4},{4,0},{8,12},{12,8},{16,20},{20,16},{24,28},{28,24},{1,5},{5... | collective-permute-start | bytes 7077896 | tf_op jit(solution)/shard_map/ppermute | solution.py:489
  320.9 12.6 %collective-permute-start.41 = (bf16[768,1536]{1,0:T(8,128)(2,1)S(1)}, bf16[768,1536]{1,0:T(8,128)(2,1)S(1)}, u32[]{:S(2)}, u32[]{:S(2)}) collective-permute-start(bf16[768,1536]{1,0:T(8,128)(2,1)S(1)} %maximum_select_fusion.1.own), channel_id=1, source_target_pairs={{0,4},{4,0},{8,12},{12,8},{16,20},{20,16},{24,28},{28,24},{1,5},{5... | collective-permute-start | bytes 7077896 | tf_op jit(solution)/shard_map/ppermute | solution.py:489
  321.4 10.1 %collective-permute-start.36 = (bf16[196,768]{1,0:T(8,128)(2,1)S(1)}, bf16[196,768]{1,0:T(8,128)(2,1)S(1)}, u32[]{:S(2)}, u32[]{:S(2)}) collective-permute-start(bf16[196,768]{1,0:T(8,128)(2,1)S(1)} %slice.88), channel_id=1, source_target_pairs={{0,16},{4,20},{8,24},{12,28},{16,0},{20,4},{24,8},{28,12},{1,17},{... | collective-permute-start | bytes 903176 | tf_op jit(solution)/shard_map/ppermute | solution.py:489
  322.7 8.7 %collective-permute-start.37 = (bf16[192,768]{1,0:T(8,128)(2,1)S(1)}, bf16[192,768]{1,0:T(8,128)(2,1)S(1)}, u32[]{:S(2)}, u32[]{:S(2)}) collective-permute-start(bf16[192,768]{1,0:T(8,128)(2,1)S(1)} %slice.89), channel_id=1, source_target_pairs={{0,8},{4,12},{8,0},{12,4},{16,24},{20,28},{24,16},{28,20},{1,9},{5... | collective-permute-start | bytes 884744 | tf_op jit(solution)/shard_map/ppermute | solution.py:489
  331.9 14.2 %collective-permute-start.39 = (bf16[384,768]{1,0:T(8,128)(2,1)S(1)}, bf16[384,768]{1,0:T(8,128)(2,1)S(1)}, u32[]{:S(2)}, u32[]{:S(2)}) collective-permute-start(bf16[384,768]{1,0:T(8,128)(2,1)S(1)} %maximum_select_fusion.10), channel_id=1, source_target_pairs={{0,16},{4,20},{8,24},{12,28},{16,0},{20,4},{24,8},{28,12},{1,17},{... | collective-permute-start | bytes 1769480 | tf_op jit(solution)/shard_map/ppermute | solution.py:489
  332.6 14.3 %collective-permute-start.38 = (bf16[392,768]{1,0:T(8,128)(2,1)S(1)}, bf16[392,768]{1,0:T(8,128)(2,1)S(1)}, u32[]{:S(2)}, u32[]{:S(2)}) collective-permute-start(bf16[392,768]{1,0:T(8,128)(2,1)S(1)} %maximum_select_fusion.8), channel_id=1, source_target_pairs={{0,8},{4,12},{8,0},{12,4},{16,24},{20,28},{24,16},{28,20},{1,9},{5... | collective-permute-start | bytes 1806344 | tf_op jit(solution)/shard_map/ppermute | solution.py:489
  348.1 6.3 %collective-permute-start.42 = (bf16[1536,768]{1,0:T(8,128)(2,1)S(1)}, bf16[1536,768]{1,0:T(8,128)(2,1)}, u32[]{:S(2)}, u32[]{:S(2)}) collective-permute-start(bf16[1536,768]{1,0:T(8,128)(2,1)S(1)} %pad_maximum_fusion.own), channel_id=1, source_target_pairs={{0,4},{4,0},{8,12},{12,8},{16,20},{20,16},{24,28},{28,24},{1,5},{5... | collective-permute-start | bytes 7077896 | tf_op jit(solution)/shard_map/ppermute | solution.py:489
  (59 other events, 236.6 us)
where the time goes:
time: 368 us; the launch traced here: 362 us
  waiting for transfers between devices  129 us (35%)
  Pallas kernels  117 us (32%)
  starting transfers between devices  47.8 us (13%)
  local copies, waits for them, and re-layouts  37.9 us (10%)
  other arithmetic  28.4 us (8%)
    ppermute x31, waiting for transfers between devices, swap(): lax.ppermute(field, axis, [(i, i ^ 1 << b) for i in range(lax.axis_size(a...  97.1 us
    pallas_call x1, Pallas kernels, run_feed(): pl.pallas_call(functools.partial(feed_kernel, images=images), grid_spec=p...  43.2 us
    ppermute x12, waiting for transfers between devices, swap_far(): return lax.ppermute(field, 'seq', [(i, i ^ distance) for i in range(size)])  31.5 us
    unnamed x160, local copies, waits for them, and re-layouts  28.8 us
    pallas_call x3, Pallas kernels, run_attention_back(): pl.pallas_call(functools.partial(attention_back_kernel, image=image, part...  26.8 us
    ppermute x12, starting transfers between devices, swap_far(): return lax.ppermute(field, 'seq', [(i, i ^ distance) for i in range(size)])  25.6 us
    ppermute x31, starting transfers between devices, swap(): lax.ppermute(field, axis, [(i, i ^ 1 << b) for i in range(lax.axis_size(a...  22.2 us
    pallas_call x1, Pallas kernels, run_attention(): pl.pallas_call(functools.partial(attention_kernel, parts=parts), grid_spe...  18 us
  transfers between devices with their start and end apart: 43, of which 23 were waited for; matrix products, arithmetic and copies ran while one was open for 4% of the time, Pallas kernels for 18%

commit v1 on v0

--- a/solution.py
+++ b/solution.py
@@ -776,9 +776,8 @@
     feed_came, came = end(pending)
     feed = [add_low(down_keep, feed_came[0]), add_low(up_keep, feed_came[1])]
     (gated,), pending = begin([scatter_stage(feed, pair(0))], after(gated, *came))
-    mixed_came = [
-        begin([Stage([after(part, gated)], [move], list)])[1] for part, move in zip(mixed[1:], far)
-    ]
+    send_back = lambda m, *gates: begin([Stage([after(mixed[m + 1], *gates)], [far[m]], list)])[1]
+    mixed_came = {len(far) - 1: send_back(len(far) - 1, gated)}
 
     fields = (
         x,
@@ -811,8 +810,12 @@
         tokens_parts.append(part)
         small = small + image_sums if image else image_sums
         extra = []
-        if image < len(mixed_came):
-            (mixed_came[image],), extra = end(mixed_came[image], image_sums)
+        if image == 0:
+            for m in range(len(far) - 1):
+                mixed_came[m] = send_back(m, image_sums)
+        turn = len(far) - image
+        if image and turn in mixed_came:
+            (mixed_came[turn],), extra = end(mixed_came[turn], image_sums)
             gated = after(gated, *extra)
         if image == images - 2 or images == 1:
             feed, came = end(pending, image_sums)
@@ -902,9 +905,9 @@
             _, pending = begin([stage])
         markers = []
         if n == 1:
-            for m in range(mixed_left, len(mixed_came)):
+            for m in range(len(far) - images + 1):
                 (mixed_came[m],), _ = end(mixed_came[m])
-            mixed = run_place(after(info, *came), [[mixed[0]]] + [[c] for c in mixed_came])
+            mixed = run_place(after(info, *came), [[mixed[0]]] + [[mixed_came[m]] for m in range(len(far))])
             markers = [mixed]
         if n == stages - 1:
             down, up = (

time: 368 us -> 366 us (level)
  waiting for transfers between devices: 129 us -> 117 us
  starting transfers between devices: 47.8 us -> 54.9 us
    ppermute x31, starting transfers between devices: 22.2 us -> 31.1 us  [swap(): lax.ppermute(field, axis, [(i, i ^ 1 << b) for i in range(lax.axis_size(a...]
    ppermute x31, waiting for transfers between devices: 97.1 us -> 89 us  [swap(): lax.ppermute(field, axis, [(i, i ^ 1 << b) for i in range(lax.axis_size(a...]
    ppermute x12, waiting for transfers between devices: 31.5 us -> 27.8 us  [swap_far(): return lax.ppermute(field, 'seq', [(i, i ^ distance) for i in range(size)])]
    unnamed x160 -> x166, local copies, waits for them, and re-layouts: 28.8 us -> 30.3 us
  transfers between devices with their start and end apart: 43 -> 43, of which waited for: 23 -> 21; matrix products, arithmetic and copies ran while one was open for 4% -> 5% of each run, Pallas kernels for 18% -> 19%
where the time goes in v1:
time: 366 us; the launch traced here: 360 us
  Pallas kernels  118 us (32%)
  waiting for transfers between devices  117 us (32%)
  starting transfers between devices  54.9 us (15%)
  local copies, waits for them, and re-layouts  39.4 us (11%)
  other arithmetic  29 us (8%)
    ppermute x31, waiting for transfers between devices, swap(): lax.ppermute(field, axis, [(i, i ^ 1 << b) for i in range(lax.axis_size(a...  89 us
    pallas_call x1, Pallas kernels, run_feed(): pl.pallas_call(functools.partial(feed_kernel, images=images), grid_spec=p...  42.9 us
    ppermute x31, starting transfers between devices, swap(): lax.ppermute(field, axis, [(i, i ^ 1 << b) for i in range(lax.axis_size(a...  31.1 us
    unnamed x166, local copies, waits for them, and re-layouts  30.3 us
    ppermute x12, waiting for transfers between devices, swap_far(): return lax.ppermute(field, 'seq', [(i, i ^ distance) for i in range(size)])  27.8 us
    pallas_call x3, Pallas kernels, run_attention_back(): pl.pallas_call(functools.partial(attention_back_kernel, image=image, part...  26.9 us
    ppermute x12, starting transfers between devices, swap_far(): return lax.ppermute(field, 'seq', [(i, i ^ distance) for i in range(size)])  23.8 us
    pallas_call x1, Pallas kernels, run_attention(): pl.pallas_call(functools.partial(attention_kernel, parts=parts), grid_spe...  18 us
  transfers between devices with their start and end apart: 43, of which 21 were waited for; matrix products, arithmetic and copies ran while one was open for 5% of the time, Pallas kernels for 19%

profile of v1, /device:TPU:0, one launch (start us, length us, event | category | flops | bytes accessed | tf_op | source)
XLA Modules:
  0.0 360.3 jit_solution(6518385449593710534)
XLA Ops:
  0.8 2.3 constant_dynamic-slice_fusion.9
  3.1 4.0 %collective-permute-start.5 = (bf16[3,80,768]{2,1,0:T(8,128)(2,1)}, bf16[3,80,768]{2,1,0:T(8,128)(2,1)S(1)}, u32[]{:S(2)}, u32[]{:S(2)}) collective-permute-start(bf16[3,80,768]{2,1,0:T(8,128)(2,1)} %get-tuple-element.291), channel_id=1, source_target_pairs={{0,2},{1,3},{2,0},{3,1},{4,6},{5,7},{6,4},{7,5},{8,10},{9,11},{10,... | collective-permute-start | bytes 1105928 | tf_op jit(solution)/shard_map/ppermute | solution.py:594
  7.2 1.6 collective-permute-start.4
  9.4 23.7 %collective-permute-done.refs_3_ = bf16[3,80,768]{2,1,0:T(8,128)(2,1)} collective-permute-done((bf16[3,80,768]{2,1,0:T(8,128)(2,1)}, bf16[3,80,768]{2,1,0:T(8,128)(2,1)}, u32[]{:S(2)}, u32[]{:S(2)}) %collective-permute-start) | collective-permute-done | bytes 368672 | tf_op jit(solution)/shard_map/ppermute | solution.py:594
  33.1 7.4 %collective-permute-start.1 = (bf16[3,80,768]{2,1,0:T(8,128)(2,1)S(1)}, bf16[3,80,768]{2,1,0:T(8,128)(2,1)S(1)}, u32[]{:S(2)}, u32[]{:S(2)}) collective-permute-start(bf16[3,80,768]{2,1,0:T(8,128)(2,1)S(1)} %get-tuple-element.149), channel_id=1, source_target_pairs={{0,1},{1,0},{2,3},{3,2},{4,5},{5,4},{6,7},{7,6},{8,9},{9,8},{10,11... | collective-permute-start | bytes 1105928 | tf_op jit(solution)/shard_map/ppermute | solution.py:594
  40.5 1.9 collective-permute-start.2
  42.4 1.5 collective-permute-start.3
  45.2 1.3 copy-done.5
  49.0 18.0 %attention_forward.1 = (bf16[3,320,768]{2,1,0:T(8,128)(2,1)S(1)}, bf16[3,320,768]{2,1,0:T(8,128)(2,1)S(1)}, bf16[3,320,768]{2,1,0:T(8,128)(2,1)S(1)}, bf16[3,320...) custom-call(s32[4]{0:T(128)S(1)} %pad_add_fusion.info, ...), custom_call_target="tpu_custom_call" | custom-call | flops 23000000512 | bytes 1000000 | tf_op jit(solution)/shard_map/attention_forward/pallas_call | solution.py:150
  67.0 1.6 copy-done.19
  76.1 42.9 %feed.1 = (bf16[3,80,768]{2,1,0:T(8,128)(2,1)S(1)}, bf16[3,80,768]{2,1,0:T(8,128)(2,1)S(1)}, bf16[3,80,768]{2,1,0:T(8,128)(2,1)S(1)}, bf16[3,80,768]{2,1,0:T(8,1...) custom-call(s32[2]{0:T(128)S(1)} %pad_add_fusion.1.info, ...), custom_call_target="tpu_custom_call" | custom-call | flops 49450000384 | bytes 1000000 | tf_op jit(solution)/shard_map/feed/pallas_call | solution.py:273
  125.2 3.1 collective-permute-done.6
  128.4 3.4 collective-permute-done.7
  131.7 2.4 add_convert_fusion.2
  134.2 3.1 add_convert_fusion.1
  137.6 2.4 collective-permute-start.8
  140.1 1.5 collective-permute-start.9
  141.5 1.5 collective-permute-start.10
  143.2 8.8 %attention_backward.5 = (bf16[3,320,768]{2,1,0:T(8,128)(2,1)S(1)}, bf16[1,80,768]{2,1,0:T(8,128)(2,1)S(1)}, bf16[1,80,768]{2,1,0:T(8,128)(2,1)S(1)}, bf16[1,80,7...) custom-call(s32[4]{0:T(128)S(1)} %pad_add_fusion.info, ...), custom_call_target="tpu_custom_call" | custom-call | flops 12650000384 | bytes 1000000 | tf_op jit(solution)/shard_map/attention_backward/pallas_call | solution.py:393
  152.0 9.0 %attention_backward.3 = (bf16[3,320,768]{2,1,0:T(8,128)(2,1)S(1)}, bf16[1,80,768]{2,1,0:T(8,128)(2,1)S(1)}, bf16[1,80,768]{2,1,0:T(8,128)(2,1)S(1)}, bf16[1,80,7...) custom-call(s32[4]{0:T(128)S(1)} %pad_add_fusion.info, ...), custom_call_target="tpu_custom_call" | custom-call | flops 12650000384 | bytes 1000000 | tf_op jit(solution)/shard_map/attention_backward/pallas_call | solution.py:393
  161.2 6.6 %collective-permute-done.9 = bf16[768,768]{1,0:T(8,128)(2,1)S(1)} collective-permute-done((bf16[768,768]{1,0:T(8,128)(2,1)S(1)}, bf16[768,768]{1,0:T(8,128)(2,1)S(1)}, u32[]{:S(2)}, u32[]{:S(2)}) %collective-permute-start.9) | collective-permute-done | bytes 1179680 | tf_op jit(solution)/shard_map/ppermute | solution.py:489
  169.8 1.6 collective-permute-start.11
  171.9 9.0 %attention_backward.4 = (bf16[3,320,768]{2,1,0:T(8,128)(2,1)S(1)}, bf16[1,80,768]{2,1,0:T(8,128)(2,1)S(1)}, bf16[1,80,768]{2,1,0:T(8,128)(2,1)S(1)}, bf16[1,80,7...) custom-call(s32[4]{0:T(128)S(1)} %pad_add_fusion.info, ...), custom_call_target="tpu_custom_call" | custom-call | flops 12650000384 | bytes 1000000 | tf_op jit(solution)/shard_map/attention_backward/pallas_call | solution.py:393
  187.1 1.8 collective-permute-start.14
  188.9 1.4 copy-done.24
  190.2 1.4 copy-done.27
  191.6 1.4 copy-done.35
  193.0 1.4 copy-done.37
  194.4 1.4 copy-done.39
  195.7 8.1 %outer.1 = (bf16[1536,768]{1,0:T(8,128)(2,1)}, bf16[1536,768]{1,0:T(8,128)(2,1)S(1)}) custom-call(s32[2]{0:T(128)S(1)} %pad_add_fusion.1.info, bf16[960,768]{1,0:T(8,128)(2,1)S(1)} %bitcast.15, bf16[960,768]{1,0:T(8,128)(2,1)S(1)} %bitcast.16, bf16[960,768]{1,0:T(8,128)(2,1)S(1)} %copy-done.27, bf16[3,320,768]{2,1,0:T(8,128)(2,1)S(1)} %copy-done.35, ...), custom_call_target="tpu_custom_call" | custom-call | flops 10350000128 | bytes 1000000 | tf_op jit(solution)/shard_map/outer/pallas_call | solution.py:444
  203.9 3.8 %collective-permute-done.14 = bf16[384,768]{1,0:T(8,128)(2,1)S(1)} collective-permute-done((bf16[384,768]{1,0:T(8,128)(2,1)S(1)}, bf16[384,768]{1,0:T(8,128)(2,1)S(1)}, u32[]{:S(2)}, u32[]{:S(2)}) %collective-permute-start.14) | collective-permute-done | bytes 589856 | tf_op jit(solution)/shard_map/ppermute | solution.py:489
  210.8 1.7 collective-permute-start.19
  212.5 2.4 collective-permute-done.17
  215.8 2.3 add_convert_fusion
  218.2 7.0 %collective-permute-done.19 = bf16[192,768]{1,0:T(8,128)(2,1)S(1)} collective-permute-done((bf16[192,768]{1,0:T(8,128)(2,1)}, bf16[192,768]{1,0:T(8,128)(2,1)S(1)}, u32[]{:S(2)}, u32[]{:S(2)}) %collective-permute-start.19) | collective-permute-done | bytes 294944 | tf_op jit(solution)/shard_map/ppermute | solution.py:489
  229.3 3.3 collective-permute-start.22
  232.6 3.4 place.2
  236.0 7.1 %collective-permute-done.21 = bf16[384,768]{1,0:T(8,128)(2,1)} collective-permute-done((bf16[384,768]{1,0:T(8,128)(2,1)}, bf16[384,768]{1,0:T(8,128)(2,1)}, u32[]{:S(2)}, u32[]{:S(2)}) %collective-permute-start.21) | collective-permute-done | bytes 589856 | tf_op jit(solution)/shard_map/ppermute | solution.py:489
  244.4 1.7 add_convert_fusion.5
  247.7 1.3 collective-permute-start.24
  249.0 2.8 collective-permute-start.25
  251.8 2.6 collective-permute-done.24
  256.0 6.6 %collective-permute-done.25 = bf16[384,768]{1,0:T(8,128)(2,1)S(1)} collective-permute-done((bf16[384,768]{1,0:T(8,128)(2,1)S(1)}, bf16[384,768]{1,0:T(8,128)(2,1)S(1)}, u32[]{:S(2)}, u32[]{:S(2)}) %collective-permute-start.25) | collective-permute-done | bytes 589856 | tf_op jit(solution)/shard_map/ppermute | solution.py:489
  264.0 1.3 reshape.96
  265.3 1.8 collective-permute-start.26
  267.1 2.0 collective-permute-start.30
  269.1 1.5 collective-permute-start.28
  271.4 5.9 %collective-permute-done.26 = bf16[194,768]{1,0:T(8,128)(2,1)} collective-permute-done((bf16[194,768]{1,0:T(8,128)(2,1)S(1)}, bf16[194,768]{1,0:T(8,128)(2,1)}, u32[]{:S(2)}, u32[]{:S(2)}) %collective-permute-start.26) | collective-permute-done | bytes 298016 | tf_op jit(solution)/shard_map/ppermute | solution.py:489
  277.3 1.4 add_convert_fusion.10
  279.5 9.2 %collective-permute-done.27 = bf16[97,768]{1,0:T(8,128)(2,1)S(1)} collective-permute-done((bf16[97,768]{1,0:T(8,128)(2,1)S(1)}, bf16[97,768]{1,0:T(8,128)(2,1)S(1)}, u32[]{:S(2)}, u32[]{:S(2)}) %collective-permute-start.27) | collective-permute-done | bytes 149024 | tf_op jit(solution)/shard_map/ppermute | solution.py:489
  288.8 1.6 maximum_select_fusion.4
  290.5 1.7 maximum_select_fusion.5
  293.1 1.5 collective-permute-start.34
  294.6 8.1 %collective-permute-done.31 = bf16[97,768]{1,0:T(8,128)(2,1)S(1)} collective-permute-done((bf16[97,768]{1,0:T(8,128)(2,1)S(1)}, bf16[97,768]{1,0:T(8,128)(2,1)S(1)}, u32[]{:S(2)}, u32[]{:S(2)}) %collective-permute-start.31) | collective-permute-done | bytes 149024 | tf_op jit(solution)/shard_map/ppermute | solution.py:489
  303.0 2.4 collective-permute-start.35
  305.4 7.7 %collective-permute-done.32 = bf16[194,768]{1,0:T(8,128)(2,1)S(1)} collective-permute-done((bf16[194,768]{1,0:T(8,128)(2,1)S(1)}, bf16[194,768]{1,0:T(8,128)(2,1)S(1)}, u32[]{:S(2)}, u32[]{:S(2)}) %collective-permute-start.32) | collective-permute-done | bytes 298016 | tf_op jit(solution)/shard_map/ppermute | solution.py:489
  313.4 4.1 %collective-permute-done.35.refs_4_ = bf16[3,80,768]{2,1,0:T(8,128)(2,1)S(1)} collective-permute-done((bf16[3,80,768]{2,1,0:T(8,128)(2,1)S(1)}, bf16[3,80,768]{2,1,0:T(8,128)(2,1)S(1)}, u32[]{:S(2)}, u32[]{:S(2)}) %collective-permute-start.35) | collective-permute-done | bytes 368672 | tf_op jit(solution)/shard_map/ppermute | solution.py:594
  319.5 1.3 collective-permute-start.36
  321.8 7.7 %collective-permute-done.37 = bf16[192,768]{1,0:T(8,128)(2,1)S(1)} collective-permute-done((bf16[192,768]{1,0:T(8,128)(2,1)S(1)}, bf16[192,768]{1,0:T(8,128)(2,1)S(1)}, u32[]{:S(2)}, u32[]{:S(2)}) %collective-permute-start.37) | collective-permute-done | bytes 294944 | tf_op jit(solution)/shard_map/ppermute | solution.py:489
  331.7 4.5 %spread.2 = f32[3072,768]{1,0:T(8,128)} custom-call(s32[2]{0:T(128)S(1)} %pad_add_fusion.1.info, bf16[1536,768]{1,0:T(8,128)(2,1)S(1)} %maximum_select_fusion.own, bf16[1536,768]{1,0:T(8,128)(2,1)S(1)} %collective-permute-done.40.other), custom_call_target="tpu_custom_call" | custom-call | flops 8049999872 | bytes 1000000 | tf_op jit(solution)/shard_map/spread/pallas_call | solution.py:529
  336.2 4.5 %spread.3 = f32[768,3072]{1,0:T(8,128)} custom-call(s32[2]{0:T(128)S(1)} %pad_add_fusion.1.info, bf16[768,1536]{1,0:T(8,128)(2,1)S(1)} %maximum_select_fusion.1.own, bf16[768,1536]{1,0:T(8,128)(2,1)S(1)} %collective-permute-done.41.other), custom_call_target="tpu_custom_call" | custom-call | flops 8049999872 | bytes 1000000 | tf_op jit(solution)/shard_map/spread/pallas_call | solution.py:529
  340.7 3.4 collective-permute-done.39
  350.2 2.2 place.3
  352.4 7.4 %split.1 = (f32[768,768]{1,0:T(8,128)}, f32[768,768]{1,0:T(8,128)}, f32[768,768]{1,0:T(8,128)}, f32[768,768]{1,0:T(8,128)}) custom-call(s32[2]{0:T(128)S(1)} %pad_add_fusion.1.info, bf16[1536,768]{1,0:T(8,128)(2,1)S(1)} %pad_maximum_fusion.own, bf16[1536,768]{1,0:T(8,128)(2,1)} %collective-permute-done.42.other), custom_call_target="tpu_custom_call" | custom-call | flops 9200000000 | bytes 1000000 | tf_op jit(solution)/shard_map/split/pallas_call | solution.py:570
  (276 shorter events, 55.3 us)
Async XLA Ops:
  3.1 40.8 %collective-permute-start.5 = (bf16[3,80,768]{2,1,0:T(8,128)(2,1)}, bf16[3,80,768]{2,1,0:T(8,128)(2,1)S(1)}, u32[]{:S(2)}, u32[]{:S(2)}) collective-permute-start(bf16[3,80,768]{2,1,0:T(8,128)(2,1)} %get-tuple-element.291), channel_id=1, source_target_pairs={{0,2},{1,3},{2,0},{3,1},{4,6},{5,7},{6,4},{7,5},{8,10},{9,11},{10,... | collective-permute-start | bytes 1105928 | tf_op jit(solution)/shard_map/ppermute | solution.py:594
  7.2 36.7 %collective-permute-start.4 = (bf16[3,80,768]{2,1,0:T(8,128)(2,1)}, bf16[3,80,768]{2,1,0:T(8,128)(2,1)}, u32[]{:S(2)}, u32[]{:S(2)}) collective-permute-start(bf16[3,80,768]{2,1,0:T(8,128)(2,1)} %get-tuple-element.292), channel_id=1, source_target_pairs={{0,1},{1,0},{2,3},{3,2},{4,5},{5,4},{6,7},{7,6},{8,9},{9,8},{10,11... | collective-permute-start | bytes 1105928 | tf_op jit(solution)/shard_map/ppermute | solution.py:594
  8.8 24.3 %collective-permute-start = (bf16[3,80,768]{2,1,0:T(8,128)(2,1)}, bf16[3,80,768]{2,1,0:T(8,128)(2,1)}, u32[]{:S(2)}, u32[]{:S(2)}) collective-permute-start(bf16[3,80,768]{2,1,0:T(8,128)(2,1)} %get-tuple-element.293), channel_id=1, source_target_pairs={{0,3},{1,2},{2,1},{3,0},{4,7},{5,6},{6,5},{7,4},{8,11},{9,10},{10,... | collective-permute-start | bytes 1105928 | tf_op jit(solution)/shard_map/ppermute | solution.py:594
  8.9 35.0 %copy-start = (bf16[12,80,768]{2,1,0:T(8,128)(2,1)S(1)}, bf16[12,80,768]{2,1,0:T(8,128)(2,1)}, u32[]{:S(2)}) copy-start(bf16[12,80,768]{2,1,0:T(8,128)(2,1)} %refs_0_.2) | copy-start | bytes 4423684
  33.1 43.0 %copy-start.2 = (bf16[12,80,768]{2,1,0:T(8,128)(2,1)S(1)}, bf16[12,80,768]{2,1,0:T(8,128)(2,1)}, u32[]{:S(2)}) copy-start(bf16[12,80,768]{2,1,0:T(8,128)(2,1)} %refs_0_.3) | copy-start | bytes 4423684
  33.1 43.0 %collective-permute-start.1 = (bf16[3,80,768]{2,1,0:T(8,128)(2,1)S(1)}, bf16[3,80,768]{2,1,0:T(8,128)(2,1)S(1)}, u32[]{:S(2)}, u32[]{:S(2)}) collective-permute-start(bf16[3,80,768]{2,1,0:T(8,128)(2,1)S(1)} %get-tuple-element.149), channel_id=1, source_target_pairs={{0,1},{1,0},{2,3},{3,2},{4,5},{5,4},{6,7},{7,6},{8,9},{9,8},{10,11... | collective-permute-start | bytes 1105928 | tf_op jit(solution)/shard_map/ppermute | solution.py:594
  40.5 35.6 %collective-permute-start.2 = (bf16[3,80,768]{2,1,0:T(8,128)(2,1)S(1)}, bf16[3,80,768]{2,1,0:T(8,128)(2,1)S(1)}, u32[]{:S(2)}, u32[]{:S(2)}) collective-permute-start(bf16[3,80,768]{2,1,0:T(8,128)(2,1)S(1)} %get-tuple-element.150), channel_id=1, source_target_pairs={{0,2},{1,3},{2,0},{3,1},{4,6},{5,7},{6,4},{7,5},{8,10},{9,11},{10,... | collective-permute-start | bytes 1105928 | tf_op jit(solution)/shard_map/ppermute | solution.py:594
  42.4 33.7 %collective-permute-start.3 = (bf16[3,80,768]{2,1,0:T(8,128)(2,1)S(1)}, bf16[3,80,768]{2,1,0:T(8,128)(2,1)S(1)}, u32[]{:S(2)}, u32[]{:S(2)}) collective-permute-start(bf16[3,80,768]{2,1,0:T(8,128)(2,1)S(1)} %get-tuple-element.151), channel_id=1, source_target_pairs={{0,3},{1,2},{2,1},{3,0},{4,7},{5,6},{6,5},{7,4},{8,11},{9,10},{10,... | collective-permute-start | bytes 1105928 | tf_op jit(solution)/shard_map/ppermute | solution.py:594
  123.5 10.7 %copy-start.15 = (bf16[3,80,768]{2,1,0:T(8,128)(2,1)}, bf16[3,80,768]{2,1,0:T(8,128)(2,1)S(1)}, u32[]{:S(2)}) copy-start(bf16[3,80,768]{2,1,0:T(8,128)(2,1)S(1)} %get-tuple-element.196) | copy-start | bytes 1105924
  123.5 4.9 %collective-permute-start.6 = (bf16[1536,768]{1,0:T(8,128)(2,1)}, bf16[1536,768]{1,0:T(8,128)(2,1)}, u32[]{:S(2)}, u32[]{:S(2)}) collective-permute-start(bf16[1536,768]{1,0:T(8,128)(2,1)} %get-tuple-element.161), channel_id=1, source_target_pairs={{0,4},{4,0},{8,12},{12,8},{16,20},{20,16},{24,28},{28,24},{1,5},{5... | collective-permute-start | bytes 7077896 | tf_op jit(solution)/shard_map/ppermute | solution.py:489
  123.5 8.2 %collective-permute-start.7 = (bf16[768,1536]{1,0:T(8,128)(2,1)}, bf16[768,1536]{1,0:T(8,128)(2,1)}, u32[]{:S(2)}, u32[]{:S(2)}) collective-permute-start(bf16[768,1536]{1,0:T(8,128)(2,1)} %get-tuple-element.162), channel_id=1, source_target_pairs={{0,4},{4,0},{8,12},{12,8},{16,20},{20,16},{24,28},{28,24},{1,5},{5... | collective-permute-start | bytes 7077896 | tf_op jit(solution)/shard_map/ppermute | solution.py:489
  125.2 55.8 %copy-start.68 = (f32[4,768]{1,0:T(4,128)}, f32[4,768]{1,0:T(4,128)S(1)}, u32[]{:S(2)}) copy-start(f32[4,768]{1,0:T(4,128)S(1)} %reshape.95) | copy-start | bytes 36868
  125.2 55.8 %copy-start.70 = (f32[3,768]{1,0:T(4,128)}, f32[3,768]{1,0:T(4,128)S(1)}, u32[]{:S(2)}) copy-start(f32[3,768]{1,0:T(4,128)S(1)} %slice.62) | copy-start | bytes 27652
  131.7 11.3 %copy-start.43 = (bf16[3,320,768]{2,1,0:T(8,128)(2,1)S(1)}, bf16[3,320,768]{2,1,0:T(8,128)(2,1)}, u32[]{:S(2)}) copy-start(bf16[3,320,768]{2,1,0:T(8,128)(2,1)} %copy-done.42) | copy-start | bytes 4423684
  131.7 11.3 %copy-start.45 = (bf16[3,320,768]{2,1,0:T(8,128)(2,1)S(1)}, bf16[3,320,768]{2,1,0:T(8,128)(2,1)}, u32[]{:S(2)}) copy-start(bf16[3,320,768]{2,1,0:T(8,128)(2,1)} %copy-done.44) | copy-start | bytes 4423684
  131.7 11.3 %copy-start.47 = (bf16[3,320,768]{2,1,0:T(8,128)(2,1)S(1)}, bf16[3,320,768]{2,1,0:T(8,128)(2,1)}, u32[]{:S(2)}) copy-start(bf16[3,320,768]{2,1,0:T(8,128)(2,1)} %copy-done.46) | copy-start | bytes 4423684
  131.7 11.3 %copy-start.55 = (f32[3,320,128]{2,1,0:T(8,128)S(1)}, f32[3,320,128]{2,1,0:T(8,128)}, u32[]{:S(2)}) copy-start(f32[3,320,128]{2,1,0:T(8,128)} %copy-done.54) | copy-start | bytes 1474564
  134.2 8.9 %copy-start.21 = (bf16[3,320,768]{2,1,0:T(8,128)(2,1)S(1)}, bf16[3,320,768]{2,1,0:T(8,128)(2,1)}, u32[]{:S(2)}) copy-start(bf16[3,320,768]{2,1,0:T(8,128)(2,1)} %copy-done.20) | copy-start | bytes 4423684
  134.2 8.9 %copy-start.26 = (bf16[960,768]{1,0:T(8,128)(2,1)S(1)}, bf16[960,768]{1,0:T(8,128)(2,1)}, u32[]{:S(2)}) copy-start(bf16[960,768]{1,0:T(8,128)(2,1)} %copy-done.25) | copy-start | bytes 4423684
  134.2 8.9 %copy-start.29 = (bf16[960,768]{1,0:T(8,128)(2,1)S(1)}, bf16[960,768]{1,0:T(8,128)(2,1)}, u32[]{:S(2)}) copy-start(bf16[960,768]{1,0:T(8,128)(2,1)} %copy-done.28) | copy-start | bytes 4423684
  137.6 23.5 %collective-permute-start.8 = (bf16[3,80,768]{2,1,0:T(8,128)(2,1)S(1)}, bf16[3,80,768]{2,1,0:T(8,128)(2,1)S(1)}, u32[]{:S(2)}, u32[]{:S(2)}) collective-permute-start(bf16[3,80,768]{2,1,0:T(8,128)(2,1)S(1)} %copy-done.18), channel_id=1, source_target_pairs={{0,3},{1,2},{2,1},{3,0},{4,7},{5,6},{6,5},{7,4},{8,11},{9,10},{10,... | collective-permute-start | bytes 1105928 | tf_op jit(solution)/shard_map/ppermute | solution.py:594
  140.1 27.7 %collective-permute-start.9 = (bf16[768,768]{1,0:T(8,128)(2,1)S(1)}, bf16[768,768]{1,0:T(8,128)(2,1)S(1)}, u32[]{:S(2)}, u32[]{:S(2)}) collective-permute-start(bf16[768,768]{1,0:T(8,128)(2,1)S(1)} %constant_dynamic-slice_fusion.8), channel_id=1, source_target_pairs={{0,8},{4,12},{8,0},{12,4},{16,24},{20,28},{24,16},{28,20},{1,9},{5... | collective-permute-start | bytes 3538952 | tf_op jit(solution)/shard_map/ppermute | solution.py:489
  141.5 27.4 %collective-permute-start.10 = (bf16[384,1536]{1,0:T(8,128)(2,1)S(1)}, bf16[384,1536]{1,0:T(8,128)(2,1)S(1)}, u32[]{:S(2)}, u32[]{:S(2)}) collective-permute-start(bf16[384,1536]{1,0:T(8,128)(2,1)S(1)} %constant_dynamic-slice_fusion.7), channel_id=1, source_target_pairs={{0,16},{4,20},{8,24},{12,28},{16,0},{20,4},{24,8},{28,12},{1,17},{... | collective-permute-start | bytes 3538952 | tf_op jit(solution)/shard_map/ppermute | solution.py:489
  152.0 9.0 %copy-start.34 = (bf16[3,320,768]{2,1,0:T(8,128)(2,1)}, bf16[3,320,768]{2,1,0:T(8,128)(2,1)S(1)}, u32[]{:S(2)}) copy-start(bf16[3,320,768]{2,1,0:T(8,128)(2,1)S(1)} %get-tuple-element.204.refs_0_) | copy-start | bytes 4423684
  152.0 9.0 %copy-start.48 = (bf16[1,80,768]{2,1,0:T(8,128)(2,1)}, bf16[1,80,768]{2,1,0:T(8,128)(2,1)S(1)}, u32[]{:S(2)}) copy-start(bf16[1,80,768]{2,1,0:T(8,128)(2,1)S(1)} %get-tuple-element.271.refs_0_) | copy-start | bytes 368644
  152.0 9.1 %copy-start.16 = (bf16[3,80,768]{2,1,0:T(8,128)(2,1)S(1)}, bf16[3,80,768]{2,1,0:T(8,128)(2,1)}, u32[]{:S(2)}) copy-start(bf16[3,80,768]{2,1,0:T(8,128)(2,1)} %copy-done.15) | copy-start | bytes 1105924
  161.1 19.9 %collective-permute-start.13 = (bf16[3,80,768]{2,1,0:T(8,128)(2,1)S(1)}, bf16[3,80,768]{2,1,0:T(8,128)(2,1)S(1)}, u32[]{:S(2)}, u32[]{:S(2)}) collective-permute-start(bf16[3,80,768]{2,1,0:T(8,128)(2,1)S(1)} %copy-done.16), channel_id=1, source_target_pairs={{0,2},{1,3},{2,0},{3,1},{4,6},{5,7},{6,4},{7,5},{8,10},{9,11},{10,... | collective-permute-start | bytes 1105928 | tf_op jit(solution)/shard_map/ppermute | solution.py:594
  169.8 14.0 %collective-permute-start.11 = (bf16[384,768]{1,0:T(8,128)(2,1)S(1)}, bf16[384,768]{1,0:T(8,128)(2,1)S(1)}, u32[]{:S(2)}, u32[]{:S(2)}) collective-permute-start(bf16[384,768]{1,0:T(8,128)(2,1)S(1)} %constant_dynamic-slice_fusion.6), channel_id=1, source_target_pairs={{0,16},{4,20},{8,24},{12,28},{16,0},{20,4},{24,8},{28,12},{1,17},{... | collective-permute-start | bytes 1769480 | tf_op jit(solution)/shard_map/ppermute | solution.py:489
  171.4 13.6 %collective-permute-start.12 = (bf16[192,1536]{1,0:T(8,128)(2,1)S(1)}, bf16[192,1536]{1,0:T(8,128)(2,1)S(1)}, u32[]{:S(2)}, u32[]{:S(2)}) collective-permute-start(bf16[192,1536]{1,0:T(8,128)(2,1)S(1)} %constant_dynamic-slice_fusion.5), channel_id=1, source_target_pairs={{0,8},{4,12},{8,0},{12,4},{16,24},{20,28},{24,16},{28,20},{1,9},{5... | collective-permute-start | bytes 1769480 | tf_op jit(solution)/shard_map/ppermute | solution.py:489
  186.8 17.1 %collective-permute-start.15 = (bf16[3,80,768]{2,1,0:T(8,128)(2,1)}, bf16[3,80,768]{2,1,0:T(8,128)(2,1)S(1)}, u32[]{:S(2)}, u32[]{:S(2)}) collective-permute-start(bf16[3,80,768]{2,1,0:T(8,128)(2,1)} %get-tuple-element.212), channel_id=1, source_target_pairs={{0,1},{1,0},{2,3},{3,2},{4,5},{5,4},{6,7},{7,6},{8,9},{9,8},{10,11... | collective-permute-start | bytes 1105928 | tf_op jit(solution)/shard_map/ppermute | solution.py:594
  187.1 20.6 %collective-permute-start.14 = (bf16[384,768]{1,0:T(8,128)(2,1)S(1)}, bf16[384,768]{1,0:T(8,128)(2,1)S(1)}, u32[]{:S(2)}, u32[]{:S(2)}) collective-permute-start(bf16[384,768]{1,0:T(8,128)(2,1)S(1)} %fusion.3), channel_id=1, source_target_pairs={{0,1},{1,0},{2,3},{3,2},{4,5},{5,4},{6,7},{7,6},{8,9},{9,8},{10,11... | collective-permute-start | bytes 1769480 | tf_op jit(solution)/shard_map/ppermute | solution.py:489
  195.7 11.9 %copy-start.57 = (bf16[384,768]{1,0:T(8,128)(2,1)S(1)}, bf16[384,768]{1,0:T(8,128)(2,1)}, u32[]{:S(2)}) copy-start(bf16[384,768]{1,0:T(8,128)(2,1)} %copy-done.56) | copy-start | bytes 1769476
  195.7 11.9 %copy-start.59 = (bf16[384,768]{1,0:T(8,128)(2,1)S(1)}, bf16[384,768]{1,0:T(8,128)(2,1)}, u32[]{:S(2)}) copy-start(bf16[384,768]{1,0:T(8,128)(2,1)} %copy-done.58) | copy-start | bytes 1769476
  203.9 11.1 %copy-start.69 = (f32[4,768]{1,0:T(4,128)S(1)}, f32[4,768]{1,0:T(4,128)}, u32[]{:S(2)}) copy-start(f32[4,768]{1,0:T(4,128)} %copy-done.68) | copy-start | bytes 36868
  203.9 11.1 %copy-start.71 = (f32[3,768]{1,0:T(4,128)S(1)}, f32[3,768]{1,0:T(4,128)}, u32[]{:S(2)}) copy-start(f32[3,768]{1,0:T(4,128)} %copy-done.70) | copy-start | bytes 27652
  210.0 5.0 %collective-permute-start.16 = (bf16[1536,768]{1,0:T(8,128)(2,1)}, bf16[1536,768]{1,0:T(8,128)(2,1)}, u32[]{:S(2)}, u32[]{:S(2)}) collective-permute-start(bf16[1536,768]{1,0:T(8,128)(2,1)} %get-tuple-element.214), channel_id=1, source_target_pairs={{0,4},{4,0},{8,12},{12,8},{16,20},{20,16},{24,28},{28,24},{1,5},{5... | collective-permute-start | bytes 7077896 | tf_op jit(solution)/shard_map/ppermute | solution.py:489
  210.0 4.9 %collective-permute-start.17 = (f32[16,768]{1,0:T(8,128)}, f32[16,768]{1,0:T(8,128)}, u32[]{:S(2)}, u32[]{:S(2)}) collective-permute-start(f32[16,768]{1,0:T(8,128)} %select_maximum_fusion), channel_id=1, source_target_pairs={{0,4},{4,0},{8,12},{12,8},{16,20},{20,16},{24,28},{28,24},{1,5},{5... | collective-permute-start | bytes 147464 | tf_op jit(solution)/shard_map/ppermute | solution.py:489
  210.5 18.8 %collective-permute-start.18 = (bf16[3,80,768]{2,1,0:T(8,128)(2,1)S(1)}, bf16[3,80,768]{2,1,0:T(8,128)(2,1)}, u32[]{:S(2)}, u32[]{:S(2)}) collective-permute-start(bf16[3,80,768]{2,1,0:T(8,128)(2,1)S(1)} %get-tuple-element.221), channel_id=1, source_target_pairs={{0,1},{1,0},{2,3},{3,2},{4,5},{5,4},{6,7},{7,6},{8,9},{9,8},{10,11... | collective-permute-start | bytes 1105928 | tf_op jit(solution)/shard_map/ppermute | solution.py:594
  210.8 14.4 %collective-permute-start.19 = (bf16[192,768]{1,0:T(8,128)(2,1)}, bf16[192,768]{1,0:T(8,128)(2,1)S(1)}, u32[]{:S(2)}, u32[]{:S(2)}) collective-permute-start(bf16[192,768]{1,0:T(8,128)(2,1)} %constant_dynamic-slice_fusion.4), channel_id=1, source_target_pairs={{0,2},{1,3},{2,0},{3,1},{4,6},{5,7},{6,4},{7,5},{8,10},{9,11},{10,... | collective-permute-start | bytes 884744 | tf_op jit(solution)/shard_map/ppermute | solution.py:489
  218.2 9.0 %copy-start.60 = (bf16[768,768]{1,0:T(8,128)(2,1)}, bf16[768,768]{1,0:T(8,128)(2,1)S(1)}, u32[]{:S(2)}) copy-start(bf16[768,768]{1,0:T(8,128)(2,1)S(1)} %get-tuple-element.289) | copy-start | bytes 3538948
  228.0 15.1 %collective-permute-start.20 = (bf16[392,768]{1,0:T(8,128)(2,1)}, bf16[392,768]{1,0:T(8,128)(2,1)}, u32[]{:S(2)}, u32[]{:S(2)}) collective-permute-start(bf16[392,768]{1,0:T(8,128)(2,1)} %fusion), channel_id=1, source_target_pairs={{0,8},{4,12},{8,0},{12,4},{16,24},{20,28},{24,16},{28,20},{1,9},{5... | collective-permute-start | bytes 1806344 | tf_op jit(solution)/shard_map/ppermute | solution.py:489
  228.7 14.4 %collective-permute-start.21 = (bf16[384,768]{1,0:T(8,128)(2,1)}, bf16[384,768]{1,0:T(8,128)(2,1)}, u32[]{:S(2)}, u32[]{:S(2)}) collective-permute-start(bf16[384,768]{1,0:T(8,128)(2,1)} %constant_dynamic-slice_fusion.3), channel_id=1, source_target_pairs={{0,16},{4,20},{8,24},{12,28},{16,0},{20,4},{24,8},{28,12},{1,17},{... | collective-permute-start | bytes 1769480 | tf_op jit(solution)/shard_map/ppermute | solution.py:489
  229.3 16.9 %collective-permute-start.22 = (bf16[192,768]{1,0:T(8,128)(2,1)}, bf16[192,768]{1,0:T(8,128)(2,1)S(1)}, u32[]{:S(2)}, u32[]{:S(2)}) collective-permute-start(bf16[192,768]{1,0:T(8,128)(2,1)} %add_convert_fusion.13), channel_id=1, source_target_pairs={{0,2},{1,3},{2,0},{3,1},{4,6},{5,7},{6,4},{7,5},{8,10},{9,11},{10,... | collective-permute-start | bytes 884744 | tf_op jit(solution)/shard_map/ppermute | solution.py:489
  232.6 10.6 %copy-start.61 = (bf16[768,768]{1,0:T(8,128)(2,1)S(1)}, bf16[768,768]{1,0:T(8,128)(2,1)}, u32[]{:S(2)}) copy-start(bf16[768,768]{1,0:T(8,128)(2,1)} %copy-done.60) | copy-start | bytes 3538948
  247.0 7.4 %collective-permute-start.23 = (bf16[196,768]{1,0:T(8,128)(2,1)S(1)}, bf16[196,768]{1,0:T(8,128)(2,1)S(1)}, u32[]{:S(2)}, u32[]{:S(2)}) collective-permute-start(bf16[196,768]{1,0:T(8,128)(2,1)S(1)} %constant_dynamic-slice_fusion.2), channel_id=1, source_target_pairs={{0,16},{4,20},{8,24},{12,28},{16,0},{20,4},{24,8},{28,12},{1,17},{... | collective-permute-start | bytes 903176 | tf_op jit(solution)/shard_map/ppermute | solution.py:489
  247.7 6.7 %collective-permute-start.24 = (bf16[192,768]{1,0:T(8,128)(2,1)S(1)}, bf16[192,768]{1,0:T(8,128)(2,1)S(1)}, u32[]{:S(2)}, u32[]{:S(2)}) collective-permute-start(bf16[192,768]{1,0:T(8,128)(2,1)S(1)} %constant_dynamic-slice_fusion.1), channel_id=1, source_target_pairs={{0,8},{4,12},{8,0},{12,4},{16,24},{20,28},{24,16},{28,20},{1,9},{5... | collective-permute-start | bytes 884744 | tf_op jit(solution)/shard_map/ppermute | solution.py:489
  249.0 13.6 %collective-permute-start.25 = (bf16[384,768]{1,0:T(8,128)(2,1)S(1)}, bf16[384,768]{1,0:T(8,128)(2,1)S(1)}, u32[]{:S(2)}, u32[]{:S(2)}) collective-permute-start(bf16[384,768]{1,0:T(8,128)(2,1)S(1)} %maximum_select_fusion.9), channel_id=1, source_target_pairs={{0,1},{1,0},{2,3},{3,2},{4,5},{5,4},{6,7},{7,6},{8,9},{9,8},{10,11... | collective-permute-start | bytes 1769480 | tf_op jit(solution)/shard_map/ppermute | solution.py:489
  265.3 12.0 %collective-permute-start.26 = (bf16[194,768]{1,0:T(8,128)(2,1)S(1)}, bf16[194,768]{1,0:T(8,128)(2,1)}, u32[]{:S(2)}, u32[]{:S(2)}) collective-permute-start(bf16[194,768]{1,0:T(8,128)(2,1)S(1)} %fusion.4), channel_id=1, source_target_pairs={{0,1},{1,0},{2,3},{3,2},{4,5},{5,4},{6,7},{7,6},{8,9},{9,8},{10,11... | collective-permute-start | bytes 893960 | tf_op jit(solution)/shard_map/ppermute | solution.py:489
  267.1 21.6 %collective-permute-start.30 = (bf16[3,80,768]{2,1,0:T(8,128)(2,1)}, bf16[3,80,768]{2,1,0:T(8,128)(2,1)S(1)}, u32[]{:S(2)}, u32[]{:S(2)}) collective-permute-start(bf16[3,80,768]{2,1,0:T(8,128)(2,1)} %get-tuple-element.243), channel_id=1, source_target_pairs={{0,3},{1,2},{2,1},{3,0},{4,7},{5,6},{6,5},{7,4},{8,11},{9,10},{10,... | collective-permute-start | bytes 1105928 | tf_op jit(solution)/shard_map/ppermute | solution.py:594
  269.1 19.7 %collective-permute-start.28 = (bf16[384,768]{1,0:T(8,128)(2,1)S(1)}, bf16[384,768]{1,0:T(8,128)(2,1)}, u32[]{:S(2)}, u32[]{:S(2)}) collective-permute-start(bf16[384,768]{1,0:T(8,128)(2,1)S(1)} %get-tuple-element.238), channel_id=1, source_target_pairs={{0,16},{4,20},{8,24},{12,28},{16,0},{20,4},{24,8},{28,12},{1,17},{... | collective-permute-start | bytes 1769480 | tf_op jit(solution)/shard_map/ppermute | solution.py:489
  270.6 18.3 %collective-permute-start.29 = (bf16[192,1536]{1,0:T(8,128)(2,1)S(1)}, bf16[192,1536]{1,0:T(8,128)(2,1)}, u32[]{:S(2)}, u32[]{:S(2)}) collective-permute-start(bf16[192,1536]{1,0:T(8,128)(2,1)S(1)} %reshape.96), channel_id=1, source_target_pairs={{0,8},{4,12},{8,0},{12,4},{16,24},{20,28},{24,16},{28,20},{1,9},{5... | collective-permute-start | bytes 1769480 | tf_op jit(solution)/shard_map/ppermute | solution.py:489
  278.8 9.9 %collective-permute-start.27 = (bf16[97,768]{1,0:T(8,128)(2,1)S(1)}, bf16[97,768]{1,0:T(8,128)(2,1)S(1)}, u32[]{:S(2)}, u32[]{:S(2)}) collective-permute-start(bf16[97,768]{1,0:T(8,128)(2,1)S(1)} %constant_dynamic-slice_fusion), channel_id=1, source_target_pairs={{0,2},{1,3},{2,0},{3,1},{4,6},{5,7},{6,4},{7,5},{8,10},{9,11},{10,... | collective-permute-start | bytes 446984 | tf_op jit(solution)/shard_map/ppermute | solution.py:489
  292.1 25.3 %collective-permute-start.33 = (bf16[768,768]{1,0:T(8,128)(2,1)S(1)}, bf16[768,768]{1,0:T(8,128)(2,1)S(1)}, u32[]{:S(2)}, u32[]{:S(2)}) collective-permute-start(bf16[768,768]{1,0:T(8,128)(2,1)S(1)} %maximum_select_fusion.4), channel_id=1, source_target_pairs={{0,8},{4,12},{8,0},{12,4},{16,24},{20,28},{24,16},{28,20},{1,9},{5... | collective-permute-start | bytes 3538952 | tf_op jit(solution)/shard_map/ppermute | solution.py:489
  293.1 24.3 %collective-permute-start.34 = (bf16[384,1536]{1,0:T(8,128)(2,1)S(1)}, bf16[384,1536]{1,0:T(8,128)(2,1)S(1)}, u32[]{:S(2)}, u32[]{:S(2)}) collective-permute-start(bf16[384,1536]{1,0:T(8,128)(2,1)S(1)} %maximum_select_fusion.5), channel_id=1, source_target_pairs={{0,16},{4,20},{8,24},{12,28},{16,0},{20,4},{24,8},{28,12},{1,17},{... | collective-permute-start | bytes 3538952 | tf_op jit(solution)/shard_map/ppermute | solution.py:489
  294.6 8.2 %collective-permute-start.31 = (bf16[97,768]{1,0:T(8,128)(2,1)S(1)}, bf16[97,768]{1,0:T(8,128)(2,1)S(1)}, u32[]{:S(2)}, u32[]{:S(2)}) collective-permute-start(bf16[97,768]{1,0:T(8,128)(2,1)S(1)} %add_convert_fusion.14), channel_id=1, source_target_pairs={{0,2},{1,3},{2,0},{3,1},{4,6},{5,7},{6,4},{7,5},{8,10},{9,11},{10,... | collective-permute-start | bytes 446984 | tf_op jit(solution)/shard_map/ppermute | solution.py:489
  302.9 10.2 %collective-permute-start.32 = (bf16[194,768]{1,0:T(8,128)(2,1)S(1)}, bf16[194,768]{1,0:T(8,128)(2,1)S(1)}, u32[]{:S(2)}, u32[]{:S(2)}) collective-permute-start(bf16[194,768]{1,0:T(8,128)(2,1)S(1)} %maximum_select_fusion.11), channel_id=1, source_target_pairs={{0,1},{1,0},{2,3},{3,2},{4,5},{5,4},{6,7},{7,6},{8,9},{9,8},{10,11... | collective-permute-start | bytes 893960 | tf_op jit(solution)/shard_map/ppermute | solution.py:489
  303.0 14.5 %collective-permute-start.35 = (bf16[3,80,768]{2,1,0:T(8,128)(2,1)S(1)}, bf16[3,80,768]{2,1,0:T(8,128)(2,1)S(1)}, u32[]{:S(2)}, u32[]{:S(2)}) collective-permute-start(bf16[3,80,768]{2,1,0:T(8,128)(2,1)S(1)} %pad_maximum_fusion.3), channel_id=1, source_target_pairs={{0,2},{1,3},{2,0},{3,1},{4,6},{5,7},{6,4},{7,5},{8,10},{9,11},{10,... | collective-permute-start | bytes 1105928 | tf_op jit(solution)/shard_map/ppermute | solution.py:594
  318.9 12.8 %collective-permute-start.40 = (bf16[1536,768]{1,0:T(8,128)(2,1)S(1)}, bf16[1536,768]{1,0:T(8,128)(2,1)S(1)}, u32[]{:S(2)}, u32[]{:S(2)}) collective-permute-start(bf16[1536,768]{1,0:T(8,128)(2,1)S(1)} %maximum_select_fusion.own), channel_id=1, source_target_pairs={{0,4},{4,0},{8,12},{12,8},{16,20},{20,16},{24,28},{28,24},{1,5},{5... | collective-permute-start | bytes 7077896 | tf_op jit(solution)/shard_map/ppermute | solution.py:489
  319.0 12.8 %collective-permute-start.41 = (bf16[768,1536]{1,0:T(8,128)(2,1)S(1)}, bf16[768,1536]{1,0:T(8,128)(2,1)S(1)}, u32[]{:S(2)}, u32[]{:S(2)}) collective-permute-start(bf16[768,1536]{1,0:T(8,128)(2,1)S(1)} %maximum_select_fusion.1.own), channel_id=1, source_target_pairs={{0,4},{4,0},{8,12},{12,8},{16,20},{20,16},{24,28},{28,24},{1,5},{5... | collective-permute-start | bytes 7077896 | tf_op jit(solution)/shard_map/ppermute | solution.py:489
  319.5 10.0 %collective-permute-start.36 = (bf16[196,768]{1,0:T(8,128)(2,1)S(1)}, bf16[196,768]{1,0:T(8,128)(2,1)S(1)}, u32[]{:S(2)}, u32[]{:S(2)}) collective-permute-start(bf16[196,768]{1,0:T(8,128)(2,1)S(1)} %slice.88), channel_id=1, source_target_pairs={{0,16},{4,20},{8,24},{12,28},{16,0},{20,4},{24,8},{28,12},{1,17},{... | collective-permute-start | bytes 903176 | tf_op jit(solution)/shard_map/ppermute | solution.py:489
  320.8 8.7 %collective-permute-start.37 = (bf16[192,768]{1,0:T(8,128)(2,1)S(1)}, bf16[192,768]{1,0:T(8,128)(2,1)S(1)}, u32[]{:S(2)}, u32[]{:S(2)}) collective-permute-start(bf16[192,768]{1,0:T(8,128)(2,1)S(1)} %slice.89), channel_id=1, source_target_pairs={{0,8},{4,12},{8,0},{12,4},{16,24},{20,28},{24,16},{28,20},{1,9},{5... | collective-permute-start | bytes 884744 | tf_op jit(solution)/shard_map/ppermute | solution.py:489
  329.9 14.2 %collective-permute-start.39 = (bf16[384,768]{1,0:T(8,128)(2,1)S(1)}, bf16[384,768]{1,0:T(8,128)(2,1)S(1)}, u32[]{:S(2)}, u32[]{:S(2)}) collective-permute-start(bf16[384,768]{1,0:T(8,128)(2,1)S(1)} %maximum_select_fusion.10), channel_id=1, source_target_pairs={{0,16},{4,20},{8,24},{12,28},{16,0},{20,4},{24,8},{28,12},{1,17},{... | collective-permute-start | bytes 1769480 | tf_op jit(solution)/shard_map/ppermute | solution.py:489
  330.7 14.3 %collective-permute-start.38 = (bf16[392,768]{1,0:T(8,128)(2,1)S(1)}, bf16[392,768]{1,0:T(8,128)(2,1)S(1)}, u32[]{:S(2)}, u32[]{:S(2)}) collective-permute-start(bf16[392,768]{1,0:T(8,128)(2,1)S(1)} %maximum_select_fusion.8), channel_id=1, source_target_pairs={{0,8},{4,12},{8,0},{12,4},{16,24},{20,28},{24,16},{28,20},{1,9},{5... | collective-permute-start | bytes 1806344 | tf_op jit(solution)/shard_map/ppermute | solution.py:489
  346.1 6.3 %collective-permute-start.42 = (bf16[1536,768]{1,0:T(8,128)(2,1)S(1)}, bf16[1536,768]{1,0:T(8,128)(2,1)}, u32[]{:S(2)}, u32[]{:S(2)}) collective-permute-start(bf16[1536,768]{1,0:T(8,128)(2,1)S(1)} %pad_maximum_fusion.own), channel_id=1, source_target_pairs={{0,4},{4,0},{8,12},{12,8},{16,20},{20,16},{24,28},{28,24},{1,5},{5... | collective-permute-start | bytes 7077896 | tf_op jit(solution)/shard_map/ppermute | solution.py:489
  (62 other events, 256.2 us)
